TPU v7x, 256 devices: a whole 4x4x8 slice. The times are simulated.
256 devices in a mesh: dp: 8 (over y, core), ctx: 32 (over x, z).
Axes of the slice: x: 4, y: 4, z: 8, core: 2. Of those that a mesh axis runs over, the one named last changes fastest.
Arguments:
- queries: bfloat16 [32768, 2048], P(('dp', 'ctx')), parts along dimension 0, may hold values from -5 to 5
- key_vectors: bfloat16 [32768, 512], P(('dp', 'ctx')), parts along dimension 0, may hold values from -5 to 5
- value_vectors: bfloat16 [32768, 512], P(('dp', 'ctx')), parts along dimension 0, may hold values from -1.5 to 1.5
- output_cotangent: bfloat16 [32768, 2048], P(('dp', 'ctx')), parts along dimension 0, may hold values from -1.5 to 1.5
- doc_lengths: int32 [32], P('dp'), parts along dimension 0, may hold values from 1 to 2176, 4096 in all
- span_of: int32 [256], P('dp'), parts along dimension 0, may hold values from 0 to 31, each once
Outputs:
- attention: bfloat16 [32768, 2048], P(('dp', 'ctx')), parts along dimension 0
- grad_queries: bfloat16 [32768, 2048], P(('dp', 'ctx')), parts along dimension 0
- key_gradient: bfloat16 [32768, 512], P(('dp', 'ctx')), parts along dimension 0
- value_gradient: bfloat16 [32768, 512], P(('dp', 'ctx')), parts along dimension 0
There are 8 independent parts, one for each index of `dp`. A program takes and returns all parts, laid end to end along the dimension named above; each array names one. Nothing has to cross between parts.
Inputs may be any that keep to these rules, and one draw needn't show every extreme that they name: `doc_lengths`: 4 lengths that sum to 4096; the largest is exactly 2176. `span_of`: a permutation of the blocks of the sequence.
All inputs are finite; a program needn't handle non-finite values.
Results may differ from a plain program's by a relative error of at most 0.017.
Values may be sent and summed in bfloat16 or wider, within the bound.
No kernel may reach another device: no remote copies, remote signals or barrier semaphores. Data moves between devices by JAX's collectives and lax.ppermute only.
A program may use at most 128 MiB of HBM per device.

v0:
```python
import jax
import jax.numpy as jnp
from jax import lax
from jax.sharding import PartitionSpec as P

QUERY_HEADS = 16
KEY_VALUE_HEADS = 4
HEAD_SIZE = 128


SCORE_MASK_FILL = -1e30


def doc_index(positions, doc_lengths):
    doc_ends = jnp.cumsum(doc_lengths)
    return jnp.sum((doc_ends[None, :] <= positions[:, None]).astype(jnp.int32), axis=1)


def row_places(first_row, count_of_rows, local_rows, span_of, doc_lengths):
    row_ids = first_row + jnp.arange(count_of_rows, dtype=jnp.int32)
    owners = row_ids // local_rows
    holder = owners[:, None] == jnp.arange(span_of.shape[0], dtype=jnp.int32)[None, :]
    span_ids = jnp.sum(jnp.where(holder, span_of[None, :], 0), axis=1)
    positions = span_ids * local_rows + row_ids % local_rows
    return (positions, doc_index(positions, doc_lengths))


def stride_for(local_rows):
    wide_rows = local_rows * max(1, 512 // local_rows)
    return wide_rows


def fold_rows(running, members, first_row, local_rows, step_fn):
    count_of_rows = members[0].shape[0]
    step_stride = stride_for(local_rows)
    block_count = count_of_rows // step_stride
    stacked = tuple(
        (member.reshape((block_count, step_stride) + member.shape[1:]) for member in members)
    )

    def advance(inner_state, packed):
        block_index, block_members = packed
        return (step_fn(inner_state, block_members, first_row + block_index * step_stride), None)

    running, unused = lax.scan(
        advance, running, (jnp.arange(block_count, dtype=jnp.int32), stacked)
    )
    return running


def masked_scores(heads_of_queries, block_of_keys, allowed):
    heads_of_keys = block_of_keys.reshape(block_of_keys.shape[0], KEY_VALUE_HEADS, HEAD_SIZE)
    scores = jnp.einsum(
        "qghd,rgd->ghqr", heads_of_queries, heads_of_keys, preferred_element_type=jnp.float32
    )
    return jnp.where(allowed, scores * HEAD_SIZE ** (-0.5), SCORE_MASK_FILL)


def on_device(queries, key_vectors, value_vectors, output_cotangent, doc_lengths, span_of):
    local_rows = queries.shape[0]
    query_groups = QUERY_HEADS // KEY_VALUE_HEADS
    inv_root = HEAD_SIZE ** (-0.5)
    width_of_terms = 2 * KEY_VALUE_HEADS * HEAD_SIZE
    own_start = lax.axis_index("ctx") * local_rows
    query_pos, query_doc = row_places(own_start, local_rows, local_rows, span_of, doc_lengths)
    heads_of_queries = queries.reshape(local_rows, KEY_VALUE_HEADS, query_groups, HEAD_SIZE)
    output_heads = output_cotangent.reshape(local_rows, KEY_VALUE_HEADS, query_groups, HEAD_SIZE)

    def pair_mask(first_row, count_of_rows):
        key_pos, key_doc = row_places(first_row, count_of_rows, local_rows, span_of, doc_lengths)
        return (query_doc[:, None] == key_doc[None, :]) & (key_pos[None, :] <= query_pos[:, None])

    def totals_step(running, members, first_row):
        block_of_keys = members[0]
        allowed = pair_mask(first_row, block_of_keys.shape[0])

        def measure(state_now):
            row_max, row_total = state_now
            scores = masked_scores(heads_of_queries, block_of_keys, allowed)
            new_max = jnp.maximum(row_max, jnp.max(scores, axis=-1))
            exps = jnp.where(allowed, jnp.exp(scores - new_max[..., None]), 0.0)
            return (new_max, row_total * jnp.exp(row_max - new_max) + jnp.sum(exps, axis=-1))

        return lax.cond(jnp.any(allowed), measure, lambda state_now: state_now, running)

    start_state = (
        jnp.full((KEY_VALUE_HEADS, query_groups, local_rows), SCORE_MASK_FILL, jnp.float32),
        jnp.zeros((KEY_VALUE_HEADS, query_groups, local_rows), jnp.float32),
    )
    row_max, row_total = fold_rows(
        start_state,
        (lax.all_gather(key_vectors, "ctx", axis=0, tiled=True),),
        jnp.int32(0),
        local_rows,
        totals_step,
    )
    complete_keys, complete_values = (
        lax.all_gather(key_vectors, "ctx", axis=0, tiled=True),
        lax.all_gather(value_vectors, "ctx", axis=0, tiled=True),
    )
    log_totals = row_max + jnp.log(row_total)

    def weighted_step(running, members, first_row):
        block_of_keys, block_of_values = members
        allowed = pair_mask(first_row, block_of_keys.shape[0])

        def attend(sums_now):
            scores = masked_scores(heads_of_queries, block_of_keys, allowed)
            weights = jnp.where(allowed, jnp.exp(scores - log_totals[..., None]), 0.0).astype(
                jnp.bfloat16
            )
            heads_of_values = block_of_values.reshape(
                block_of_values.shape[0], KEY_VALUE_HEADS, HEAD_SIZE
            )
            return sums_now + jnp.einsum(
                "ghqr,rgd->qghd", weights, heads_of_values, preferred_element_type=jnp.float32
            )

        return lax.cond(jnp.any(allowed), attend, lambda sums_now: sums_now, running)

    zero_sums_init = jnp.zeros((local_rows, KEY_VALUE_HEADS, query_groups, HEAD_SIZE), jnp.float32)
    weighted = fold_rows(
        zero_sums_init, (complete_keys, complete_values), 0, local_rows, weighted_step
    )
    attention = weighted.astype(jnp.bfloat16)
    out_dot = jnp.transpose(
        jnp.sum(attention.astype(jnp.float32) * output_heads.astype(jnp.float32), axis=-1),
        (1, 2, 0),
    )

    def grad_parts(block_of_keys, block_of_values, allowed):
        scores = masked_scores(heads_of_queries, block_of_keys, allowed)
        weights = jnp.where(allowed, jnp.exp(scores - log_totals[..., None]), 0.0)
        heads_of_values = block_of_values.reshape(
            block_of_values.shape[0], KEY_VALUE_HEADS, HEAD_SIZE
        )
        grad_weights = jnp.einsum(
            "qghd,rgd->ghqr", output_heads, heads_of_values, preferred_element_type=jnp.float32
        )
        grad_scores = (weights * (grad_weights - out_dot[..., None])).astype(jnp.bfloat16)
        return (weights, grad_scores)

    def kv_terms_of(weights, grad_scores, count_of_rows):
        key_gradient_part = inv_root * jnp.einsum(
            "ghqr,qghd->rgd", grad_scores, heads_of_queries, preferred_element_type=jnp.float32
        )
        value_gradient_part = jnp.einsum(
            "ghqr,qghd->rgd",
            weights.astype(jnp.bfloat16),
            output_heads,
            preferred_element_type=jnp.float32,
        )
        return jnp.concatenate(
            [
                key_gradient_part.reshape(count_of_rows, KEY_VALUE_HEADS * HEAD_SIZE),
                value_gradient_part.reshape(count_of_rows, KEY_VALUE_HEADS * HEAD_SIZE),
            ],
            axis=1,
        )

    total_rows = complete_keys.shape[0]
    step_stride = stride_for(local_rows)
    block_count = total_rows // step_stride

    def both_step(query_sums, packed):
        block_start, block_of_keys, block_of_values = packed
        allowed = pair_mask(block_start, step_stride)

        def compute(sums_now):
            weights, grad_scores = grad_parts(block_of_keys, block_of_values, allowed)
            heads_of_keys = block_of_keys.reshape(step_stride, KEY_VALUE_HEADS, HEAD_SIZE)
            sums_next = sums_now + jnp.einsum(
                "ghqr,rgd->qghd", grad_scores, heads_of_keys, preferred_element_type=jnp.float32
            )
            return (sums_next, kv_terms_of(weights, grad_scores, step_stride))

        def skip(sums_now):
            return (sums_now, jnp.zeros((step_stride, width_of_terms), jnp.float32))

        return lax.cond(jnp.any(allowed), compute, skip, query_sums)

    block_starts = jnp.arange(block_count, dtype=jnp.int32) * step_stride
    query_sums, term_blocks = lax.scan(
        both_step,
        zero_sums_init,
        (
            block_starts,
            complete_keys.reshape(block_count, step_stride, KEY_VALUE_HEADS * HEAD_SIZE),
            complete_values.reshape(block_count, step_stride, KEY_VALUE_HEADS * HEAD_SIZE),
        ),
    )
    summed_total = lax.psum_scatter(
        term_blocks.reshape(total_rows, width_of_terms).astype(jnp.bfloat16),
        "ctx",
        scatter_dimension=0,
        tiled=True,
    ).astype(jnp.float32)
    grad_queries = (
        (inv_root * query_sums).reshape(local_rows, QUERY_HEADS * HEAD_SIZE).astype(jnp.bfloat16)
    )
    key_gradient = summed_total[:, : KEY_VALUE_HEADS * HEAD_SIZE].astype(jnp.bfloat16)
    value_gradient = summed_total[:, KEY_VALUE_HEADS * HEAD_SIZE :].astype(jnp.bfloat16)
    return (
        attention.reshape(local_rows, QUERY_HEADS * HEAD_SIZE),
        grad_queries,
        key_gradient,
        value_gradient,
    )


def solution(mesh):
    placed = (
        P(("dp", "ctx"), None),
        P(("dp", "ctx"), None),
        P(("dp", "ctx"), None),
        P(("dp", "ctx"), None),
        P("dp"),
        P("dp"),
    )
    return jax.shard_map(
        on_device,
        mesh=mesh,
        in_specs=placed,
        out_specs=(
            P(("dp", "ctx"), None),
            P(("dp", "ctx"), None),
            P(("dp", "ctx"), None),
            P(("dp", "ctx"), None),
        ),
        check_vma=False,
    )
```

profile of v0, /device:TPU:1, one launch (start us, length us, event | category | flops | bytes accessed | tf_op | source)
XLA Modules:
  0.0 619.1 jit_solution(9639522740087187333)
XLA Ops:
  9.5 2.0 copy.110
  11.6 1.3 copy.102
  14.1 79.5 %all-gather.3.cloned.1.call-done = bf16[4096,512]{1,0:T(8,128)(2,1)} async-done(((bf16[128,512]{1,0:T(8,128)(2,1)}), bf16[4096,512]{1,0:T(8,128)(2,1)}) %all-gather.3.cloned.1.call-update) | async-done | bytes 4194320 | tf_op jit(solution)/shard_map/all_gather | solution.py:98
  93.5 6.5 %copy.105 = bf16[8,512,512]{1,2,0:T(8,128)(2,1)} copy(bf16[8,512,512]{2,1,0:T(8,128)(2,1)} %bitcast.153) | data formatting | bytes 8388608 | tf_op jit(solution)/shard_map/while | solution.py:45
  100.0 75.1 %all-gather.5.cloned.1.call-done = bf16[4096,512]{1,0:T(8,128)(2,1)} async-done(((bf16[128,512]{1,0:T(8,128)(2,1)}), bf16[4096,512]{1,0:T(8,128)(2,1)}) %all-gather.5.cloned.1.call-update) | async-done | bytes 4194320 | tf_op jit(solution)/shard_map/all_gather | solution.py:99
  175.1 6.5 %copy.107 = bf16[8,512,512]{1,2,0:T(8,128)(2,1)} copy(bf16[8,512,512]{2,1,0:T(8,128)(2,1)} %bitcast.154) | data formatting | bytes 8388608 | tf_op jit(solution)/shard_map/while | solution.py:45
  181.6 45.7 %while.46 = (s32[]{:T(128)}, f32[4,4,128]{2,1,0:T(4,128)S(1)}, f32[4,4,128]{2,1,0:T(4,128)S(1)}, s32[128]{0:T(128)S(1)}, s32[1,4]{1,0:T(1,128)S(1)}, /*index=5*/...) while((s32[]{:T(128)}, f32[4,4,128]{2,1,0:T(4,128)S(1)}, ...), condition=%wide.region_11.12_spmd, body=%wide.region_3.11_spmd.sunk | while | flops 277159936 | bytes 10808719 | solution.py:45
  184.7 3.0 conditional.6
  190.8 3.0 conditional.6
  200.0 3.0 conditional.6
  206.1 3.0 conditional.6
  212.2 3.0 conditional.6
  218.3 3.0 conditional.6
  224.4 3.0 conditional.6
  227.5 47.5 %while.47 = (s32[]{:T(128)}, f32[128,4,4,128]{3,0,2,1:T(8,128)S(1)}, s32[128]{0:T(128)S(1)}, s32[1,4]{1,0:T(1,128)S(1)}, s32[8]{0:T(128)S(1)}, /*index=5*/s32[32...) while((s32[]{:T(128)}, ...), condition=%wide.region_18.19_spmd, body=%wide.region_12.18_spmd.sunk | while | flops 542707712 | bytes 5926271 | solution.py:45
  230.3 3.6 conditional.7
  230.3 1.3 constant_dynamic-slice_fusion.1
  231.6 2.3 fusion.11
  236.7 3.6 conditional.7
  236.7 1.3 constant_dynamic-slice_fusion.1
  238.0 2.3 fusion.11
  245.8 3.6 conditional.7
  245.8 1.3 constant_dynamic-slice_fusion.1
  247.1 2.3 fusion.11
  252.2 3.6 conditional.7
  252.2 1.3 constant_dynamic-slice_fusion.1
  253.5 2.3 fusion.11
  258.6 3.6 conditional.7
  258.6 1.3 constant_dynamic-slice_fusion.1
  259.9 2.3 fusion.11
  265.0 3.6 conditional.7
  265.0 1.3 constant_dynamic-slice_fusion.1
  266.3 2.3 fusion.11
  271.4 3.6 conditional.7
  271.4 1.3 constant_dynamic-slice_fusion.1
  272.7 2.3 fusion.11
  275.3 1.4 multiply_reduce_fusion
  276.8 84.9 %while.48 = (s32[]{:T(128)}, f32[128,4,4,128]{3,0,2,1:T(8,128)S(1)}, bf16[8,512,1024]{1,2,0:T(8,128)(2,1)}, s32[128]{0:T(128)S(1)}, s32[1,4]{1,0:T(1,128)S(1)}, ...) while((s32[]{:T(128)}, ...), condition=%wide.region_26.27_spmd, body=%wide.region_20.26_spmd.sunk | while | flops 1357975552 | bytes 34320312 | solution.py:183
  280.1 7.1 %conditional.8 = (f32[128,4,4,128]{3,0,2,1:T(8,128)S(1)}, bf16[1,512,1024]{1,2,0:T(8,128)(2,1)S(1)}) conditional(s32[]{:T(128)} %convert_element_type.114, f32[128,4,4,128]{3,0,2,1:T(8,128)S(1)} %get-tuple-element.1216, (pred[128,512]{0,1:T(8,128)(4,1)S(1)}, bf16[8,512,512]{1,2,0:T(8,128)(2,1)}, s32[]{:T(128)}, ...), branch_computations={%region_24.24_spmd, %region_25.25_spmd} | conditional | flops 1357643776 | bytes 32137264 | solution.py:180
  280.1 1.3 constant_dynamic-slice_fusion.3
  283.5 1.6 fusion.20
  291.6 7.1 %conditional.8 = (f32[128,4,4,128]{3,0,2,1:T(8,128)S(1)}, bf16[1,512,1024]{1,2,0:T(8,128)(2,1)S(1)}) conditional(s32[]{:T(128)} %convert_element_type.114, f32[128,4,4,128]{3,0,2,1:T(8,128)S(1)} %get-tuple-element.1216, (pred[128,512]{0,1:T(8,128)(4,1)S(1)}, bf16[8,512,512]{1,2,0:T(8,128)(2,1)}, s32[]{:T(128)}, ...), branch_computations={%region_24.24_spmd, %region_25.25_spmd} | conditional | flops 1357643776 | bytes 32137264 | solution.py:180
  291.6 1.3 constant_dynamic-slice_fusion.3
  293.7 1.2 fusion.25
  294.9 1.6 fusion.20
  307.6 7.1 %conditional.8 = (f32[128,4,4,128]{3,0,2,1:T(8,128)S(1)}, bf16[1,512,1024]{1,2,0:T(8,128)(2,1)S(1)}) conditional(s32[]{:T(128)} %convert_element_type.114, f32[128,4,4,128]{3,0,2,1:T(8,128)S(1)} %get-tuple-element.1216, (pred[128,512]{0,1:T(8,128)(4,1)S(1)}, bf16[8,512,512]{1,2,0:T(8,128)(2,1)}, s32[]{:T(128)}, ...), branch_computations={%region_24.24_spmd, %region_25.25_spmd} | conditional | flops 1357643776 | bytes 32137264 | solution.py:180
  307.6 1.3 constant_dynamic-slice_fusion.3
  309.7 1.2 fusion.25
  310.9 1.6 fusion.20
  319.1 7.1 %conditional.8 = (f32[128,4,4,128]{3,0,2,1:T(8,128)S(1)}, bf16[1,512,1024]{1,2,0:T(8,128)(2,1)S(1)}) conditional(s32[]{:T(128)} %convert_element_type.114, f32[128,4,4,128]{3,0,2,1:T(8,128)S(1)} %get-tuple-element.1216, (pred[128,512]{0,1:T(8,128)(4,1)S(1)}, bf16[8,512,512]{1,2,0:T(8,128)(2,1)}, s32[]{:T(128)}, ...), branch_computations={%region_24.24_spmd, %region_25.25_spmd} | conditional | flops 1357643776 | bytes 32137264 | solution.py:180
  319.1 1.3 constant_dynamic-slice_fusion.3
  322.4 1.6 fusion.20
  330.5 7.1 %conditional.8 = (f32[128,4,4,128]{3,0,2,1:T(8,128)S(1)}, bf16[1,512,1024]{1,2,0:T(8,128)(2,1)S(1)}) conditional(s32[]{:T(128)} %convert_element_type.114, f32[128,4,4,128]{3,0,2,1:T(8,128)S(1)} %get-tuple-element.1216, (pred[128,512]{0,1:T(8,128)(4,1)S(1)}, bf16[8,512,512]{1,2,0:T(8,128)(2,1)}, s32[]{:T(128)}, ...), branch_computations={%region_24.24_spmd, %region_25.25_spmd} | conditional | flops 1357643776 | bytes 32137264 | solution.py:180
  330.6 1.3 constant_dynamic-slice_fusion.3
  333.9 1.6 fusion.20
  342.0 7.1 %conditional.8 = (f32[128,4,4,128]{3,0,2,1:T(8,128)S(1)}, bf16[1,512,1024]{1,2,0:T(8,128)(2,1)S(1)}) conditional(s32[]{:T(128)} %convert_element_type.114, f32[128,4,4,128]{3,0,2,1:T(8,128)S(1)} %get-tuple-element.1216, (pred[128,512]{0,1:T(8,128)(4,1)S(1)}, bf16[8,512,512]{1,2,0:T(8,128)(2,1)}, s32[]{:T(128)}, ...), branch_computations={%region_24.24_spmd, %region_25.25_spmd} | conditional | flops 1357643776 | bytes 32137264 | solution.py:180
  342.1 1.3 constant_dynamic-slice_fusion.3
  345.4 1.6 fusion.20
  353.5 7.1 %conditional.8 = (f32[128,4,4,128]{3,0,2,1:T(8,128)S(1)}, bf16[1,512,1024]{1,2,0:T(8,128)(2,1)S(1)}) conditional(s32[]{:T(128)} %convert_element_type.114, f32[128,4,4,128]{3,0,2,1:T(8,128)S(1)} %get-tuple-element.1216, (pred[128,512]{0,1:T(8,128)(4,1)S(1)}, bf16[8,512,512]{1,2,0:T(8,128)(2,1)}, s32[]{:T(128)}, ...), branch_computations={%region_24.24_spmd, %region_25.25_spmd} | conditional | flops 1357643776 | bytes 32137264 | solution.py:180
  353.6 1.3 constant_dynamic-slice_fusion.3
  356.9 1.6 fusion.20
  361.7 11.4 %copy.114 = bf16[8,512,1024]{2,1,0:T(8,128)(2,1)} copy(bf16[8,512,1024]{1,2,0:T(8,128)(2,1)} %get-tuple-element.652) | data formatting | bytes 16777216 | tf_op jit(solution)/shard_map/convert_element_type | solution.py:193
  376.9 233.9 %reduce-scatter.2.cloned.1.call-done = bf16[128,1024]{1,0:T(8,128)(2,1)} async-done(((bf16[4096,1024]{1,0:T(8,128)(2,1)}), bf16[128,1024]{1,0:T(8,128)(2,1)}) %reduce-scatter.2.cloned.1.call-update) | async-done | bytes 262160 | tf_op jit(solution)/shard_map/reduce_scatter | solution.py:192
  610.8 1.7 fusion.41
  (277 shorter events, 112.0 us)
Async XLA Ops:
  7.2 86.4 %all-gather.3.cloned.1.call-start = ((), (), s32[]{:S(2)}) async-start(), calls=%async_computation.1 | async-start | bytes 4325376 | tf_op jit(solution)/shard_map/all_gather | solution.py:98
  7.9 167.2 %all-gather.5.cloned.1.call-start = ((), (), s32[]{:S(2)}) async-start(), calls=%async_computation.2 | async-start | bytes 4325376 | tf_op jit(solution)/shard_map/all_gather | solution.py:99
  8.6 602.2 %reduce-scatter.2.cloned.1.call-start = ((), (), s32[]{:S(2)}) async-start(), calls=%async_computation.3 | async-start | bytes 8650752 | tf_op jit(solution)/shard_map/reduce_scatter | solution.py:192
  175.1 6.5 %copy-start.3 = (s32[32]{0:T(128)S(1)}, s32[32]{0:T(128)}, u32[]{:S(2)}) copy-start(s32[32]{0:T(128)} %param.23) | copy-start | bytes 388
  275.3 1.5 copy-start
  280.1 2.1 copy-start.2
  291.6 2.1 copy-start.2
  307.6 2.1 copy-start.2
  319.1 2.1 copy-start.2
  330.5 2.1 copy-start.2
  342.1 2.1 copy-start.2
  353.6 2.1 copy-start.2
  373.1 1.0 copy-start.1
Sparse Core Ops, SparseCore 0:
  10.6 82.8 all-gather.2
  96.1 78.9 all-gather.4
  373.3 237.5 reduce-scatter.1
where the time goes:
time: 624 us; the launch traced here: 619 us
  waiting for transfers between devices  390 us (62%)
  local copies, waits for them, and re-layouts  82.9 us (13%)
  matrix products  61.5 us (10%)
  other arithmetic  45 us (7%)
  loops' own time  25.8 us (4%)
  between operations  13.9 us (2%)
    reduce_scatter x1, waiting for transfers between devices, on_device(): lax.psum_scatter(term_blocks.reshape(total_rows, width_of_terms).astype(j...  234 us
    all_gather x1, waiting for transfers between devices, on_device(): lax.all_gather(key_vectors, 'ctx', axis=0, tiled=True)  79.5 us
    all_gather x1, waiting for transfers between devices, on_device(): lax.all_gather(value_vectors, 'ctx', axis=0, tiled=True)  75.1 us
    dynamic_slice x45, local copies, waits for them, and re-layouts, fold_rows(): lax.scan(advance, running, (jnp.arange(block_count, dtype=jnp.int32), sta...  40.4 us
    another operation x2, loops' own time, fold_rows(): lax.scan(advance, running, (jnp.arange(block_count, dtype=jnp.int32), sta...  20.1 us
    dot_general x7, matrix products, attend(): jnp.einsum('ghqr,rgd->qghd', weights, heads_of_values, preferred_element_...  16.1 us
    while x4, local copies, waits for them, and re-layouts, fold_rows(): lax.scan(advance, running, (jnp.arange(block_count, dtype=jnp.int32), sta...  13.5 us
  transfers between devices with their start and end apart: 3, of which 3 were waited for; matrix products, arithmetic and copies ran while one was open for 2% of the time, Pallas kernels for 0%

commit v1 on v0

v1 whole, which is shorter than its diff:
```python
import functools

import jax
import jax.numpy as jnp
from jax import lax
from jax.experimental import pallas as pl
from jax.experimental.pallas import tpu as pltpu
from jax.sharding import Mesh, PartitionSpec as P

HEADS = 4
D = 128
B = 128
NX, NZ = 4, 8
NB = NX * NZ
W = HEADS * B
CHUNKS = 9
SCALE = D ** -0.5
SCALE_LOG2 = SCALE * 1.4426950408889634
FILL = -1e30
BF, F32 = jnp.bfloat16, jnp.float32


def nt(a, b):
    return lax.dot_general(a, b, (((1,), (1,)), ((), ())), preferred_element_type=F32)


def tn(a, b):
    return lax.dot_general(a, b, (((0,), (0,)), ((), ())), preferred_element_type=F32)


def nn(a, b):
    return lax.dot_general(a, b, (((1,), (0,)), ((), ())), preferred_element_type=F32)


def attention_kernel(span_ref, doc_ref, z_ref, q_ref, do_ref, kv_ref,
                     o_ref, dq_ref, dkv_ref, p_ref, acc_ref, slot_ref, pb_ref):
    z = z_ref[0]
    ends = []
    total = jnp.int32(0)
    for i in range(4):
        total = total + doc_ref[i]
        ends.append(total)

    def place(i, carry):
        slot_ref[span_ref[i]] = lax.rem(i, NZ) * NX + i // NZ
        return carry

    lax.fori_loop(0, NB, place, 0)
    slot_ref[NB] = 0
    acc_ref[...] = jnp.zeros_like(acc_ref)

    def stacked(ref, i):
        rows = ref[i]
        return jnp.concatenate([rows[:, h * D:(h + 1) * D] for h in range(HEADS)], axis=0)

    def one_block(i, carry):
        span = span_ref[i * NZ + z]
        first = span * B
        start_first = jnp.int32(0)
        lane = lax.broadcasted_iota(jnp.int32, (1, W), 1)
        q_pos = first + lax.rem(lane, B)
        q_start = jnp.zeros((1, W), jnp.int32)
        start_last = jnp.int32(0)
        for e in ends:
            start_first = jnp.where(e <= first, e, start_first)
            start_last = jnp.where(e <= first + B - 1, e, start_last)
            q_start = jnp.where(e <= q_pos, e, q_start)
        low = start_first // B
        count = (span - low) // 2 + 1
        qs = stacked(q_ref, i)

        def pair(c):
            s = low + 2 * c
            return s, slot_ref[s], slot_ref[s + 1]

        def keys(a, b):
            return jnp.concatenate([kv_ref[a, :, :D], kv_ref[b, :, :D]], axis=0)

        def values(a, b):
            return jnp.concatenate([kv_ref[a, :, D:], kv_ref[b, :, D:]], axis=0)

        def score_step(c, m):
            s, a, b = pair(c)
            st = nt(keys(a, b), qs) * SCALE_LOG2
            k_pos = s * B + lax.broadcasted_iota(jnp.int32, (2 * B, W), 0)
            st = jnp.where((k_pos >= q_start) & (k_pos <= q_pos), st, FILL)
            p_ref[c] = st
            return jnp.maximum(m, jnp.max(st, axis=0, keepdims=True))

        m = lax.fori_loop(0, count, score_step, jnp.full((1, W), FILL, F32))

        def weigh_step(c, state):
            l, ot = state
            s, a, b = pair(c)
            p = jnp.exp2(p_ref[c] - m)
            pb = p.astype(BF)
            pb_ref[c] = pb
            return l + jnp.sum(p, axis=0, keepdims=True), ot + tn(values(a, b), pb)

        l, ot = lax.fori_loop(
            0, count, weigh_step, (jnp.zeros((1, W), F32), jnp.zeros((D, W), F32))
        )
        inv = 1.0 / l
        ob = (ot * inv).astype(BF)
        dos = stacked(do_ref, i)
        dot = jnp.concatenate(
            [dos[h * B:(h + 1) * B, :].astype(F32).T for h in range(HEADS)], axis=1
        )
        dotn = dot * inv
        dos = jnp.concatenate(
            [dotn[:, h * B:(h + 1) * B].T for h in range(HEADS)], axis=0
        ).astype(BF)
        delta = jnp.sum(ob.astype(F32) * dotn, axis=0, keepdims=True)

        def back_step(c, dqt):
            s, a, b = pair(c)
            pb = pb_ref[c]
            dp = nt(values(a, b), dos)
            ds = (pb.astype(F32) * (dp - delta)).astype(BF)
            dv = nn(pb, dos)
            dk = nn(ds, qs)
            acc_ref[a, :, :D] += dk[:B]
            acc_ref[b, :, :D] += dk[B:]
            acc_ref[a, :, D:] += dv[:B]
            acc_ref[b, :, D:] += dv[B:]
            return dqt + tn(keys(a, b), ds)

        dqt = lax.fori_loop(0, count, back_step, jnp.zeros((D, W), F32))
        for h in range(HEADS):
            cols = slice(h * B, (h + 1) * B)
            o_ref[i, :, cols] = ob[:, cols].astype(F32).T.astype(BF)
            dq_ref[i, :, cols] = (dqt[:, cols] * SCALE).T.astype(BF)
        return carry

    lax.fori_loop(0, NX, one_block, 0)

    def put(i, carry):
        dkv_ref[i, :, :D] = (acc_ref[i, :, :D] * SCALE).astype(BF)
        dkv_ref[i, :, D:] = acc_ref[i, :, D:].astype(BF)
        return carry

    lax.fori_loop(0, NB, put, 0)


def attend(span_of, doc_lengths, z, q, do, kv):
    vm = pl.BlockSpec(memory_space=pltpu.VMEM)
    sm = pl.BlockSpec(memory_space=pltpu.SMEM)
    return pl.pallas_call(
        attention_kernel,
        in_specs=[sm, sm, sm, vm, vm, vm],
        out_specs=[vm, vm, vm],
        out_shape=[
            jax.ShapeDtypeStruct((NX, B, W), BF),
            jax.ShapeDtypeStruct((NX, B, W), BF),
            jax.ShapeDtypeStruct((NB, B, 2 * D), BF),
        ],
        scratch_shapes=[
            pltpu.VMEM((CHUNKS, 2 * B, W), F32),
            pltpu.VMEM((NB, B, 2 * D), F32),
            pltpu.SMEM((NB + 8,), jnp.int32),
            pltpu.VMEM((CHUNKS, 2 * B, W), BF),
        ],
        compiler_params=pltpu.CompilerParams(vmem_limit_bytes=48 * 2 ** 20),
        name="attention",
    )(span_of, doc_lengths, z, q, do, kv)


def on_device(queries, key_vectors, value_vectors, output_cotangent, doc_lengths, span_of):
    z = lax.axis_index("z").astype(jnp.int32).reshape(1)
    k = key_vectors.reshape(B, NX, D)
    v = value_vectors.reshape(B, NX, D)
    kv = jnp.concatenate([k, v], axis=2).transpose(1, 0, 2)
    kv = lax.all_to_all(kv, "x", 0, 0)
    kv = lax.all_gather(kv, "z", axis=0, tiled=True)
    q = lax.all_to_all(queries.reshape(B, NX, W).transpose(1, 0, 2), "x", 0, 0)
    do = lax.all_to_all(output_cotangent.reshape(B, NX, W).transpose(1, 0, 2), "x", 0, 0)
    o, dq, dkv = attend(span_of, doc_lengths, z, q, do, kv)
    dkv = lax.psum_scatter(dkv, "z", scatter_dimension=0, tiled=True)
    dkv = lax.all_to_all(dkv, "x", 0, 0)
    o = lax.all_to_all(o, "x", 0, 0).transpose(1, 0, 2).reshape(B, NX * W)
    dq = lax.all_to_all(dq, "x", 0, 0).transpose(1, 0, 2).reshape(B, NX * W)
    dkv = dkv.transpose(1, 0, 2)
    dk = dkv[:, :, :D].reshape(B, NX * D)
    dv = dkv[:, :, D:].reshape(B, NX * D)
    return o, dq, dk, dv


def solution(mesh):
    split = Mesh(mesh.devices.reshape(-1, NX, NZ), ("dp", "x", "z"))
    rows = P(("dp", "x", "z"), None)
    part = P("dp")
    return jax.shard_map(
        on_device,
        mesh=split,
        in_specs=(rows, rows, rows, rows, part, part),
        out_specs=(rows, rows, rows, rows),
        check_vma=False,
    )
```

time: 624 us -> 154 us (0.25)
  the two profiles are of different devices: /device:TPU:1 before, /device:TPU:8 now
where the time goes in v1:
time: 154 us
  waiting for transfers between devices  66.5 us (43%)
  blocking collectives  37 us (24%)
  Pallas kernels  15 us (10%)
  between operations  14.2 us (9%)
  starting transfers between devices  11.4 us (7%)
  local copies, waits for them, and re-layouts  9.96 us (6%)
    reduce_scatter x1, waiting for transfers between devices, on_device(): dkv = lax.psum_scatter(dkv, 'z', scatter_dimension=0, tiled=True)  29.8 us
    all_gather x1, waiting for transfers between devices, on_device(): kv = lax.all_gather(kv, 'z', axis=0, tiled=True)  17.5 us
    pallas_call x1, Pallas kernels, attend(): pl.pallas_call(attention_kernel, in_specs=[sm, sm, sm, vm, vm, vm], out_s...  15 us
    all_to_all x1, blocking collectives, on_device(): o = lax.all_to_all(o, 'x', 0, 0).transpose(1, 0, 2).reshape(B, NX * W)  14.5 us
    all_to_all x1, blocking collectives, on_device(): dq = lax.all_to_all(dq, 'x', 0, 0).transpose(1, 0, 2).reshape(B, NX * W)  11.8 us
    all_to_all x1, blocking collectives, on_device(): kv = lax.all_to_all(kv, 'x', 0, 0)  10.8 us
    all_to_all x1, waiting for transfers between devices, on_device(): lax.all_to_all(output_cotangent.reshape(B, NX, W).transpose(1, 0, 2), 'x'...  7.99 us
    all_to_all x1, waiting for transfers between devices, on_device(): q = lax.all_to_all(queries.reshape(B, NX, W).transpose(1, 0, 2), 'x', 0, 0)  7.02 us
  transfers between devices with their start and end apart: 5, of which 5 were waited for; matrix products, arithmetic and copies ran while one was open for 3% of the time, Pallas kernels for 0%

profile of v1, /device:TPU:8, one launch (start us, length us, event | category | flops | bytes accessed | tf_op | source)
XLA Modules:
  0.0 154.0 jit_solution(8153552590067193311)
XLA Ops:
  7.2 0.0 copy-start.2
  7.2 0.0 all-gather.2.cloned.1.call-start
  7.2 1.1 copy.30
  8.3 1.0 copy.31
  9.4 10.8 %all_to_all.30 = bf16[4,128,256]{1,2,0:T(8,128)(2,1)S(1)} all-to-all(bf16[4,128,256]{1,2,0:T(8,128)(2,1)S(1)} %maximum_bitcast_fusion), channel_id=1, replica_groups=mesh['dp'=8,'x'=4,'z'=8] {'x'}, dimensions={0} | all-to-all | bytes 524288 | tf_op jit(solution)/shard_map/all_to_all | solution.py:173
  20.1 0.0 copy-start.3
  20.1 0.8 copy.32
  21.0 0.0 all-gather.2.cloned.1.call-update
  21.0 0.0 copy-done.2
  21.0 0.3 copy.26
  21.3 1.0 copy.27
  22.3 0.0 copy-start
  22.3 0.0 copy-start.1
  22.3 3.6 %all-to-all-start = ((bf16[4,128,512]{2,1,0:T(8,128)(2,1)}), bf16[4,128,512]{2,1,0:T(8,128)(2,1)S(1)}, u32[]{:S(2)}, u32[]{:S(2)}) async-start(bf16[4,128,512]{2,1,0:T(8,128)(2,1)} %bitcast.2), calls=%async_computation | async-start | bytes 1048576 | tf_op jit(solution)/shard_map/all_to_all | solution.py:175
  25.9 0.0 copy-done.3
  25.9 0.3 copy.28
  26.2 1.0 copy.29
  27.2 7.0 %all-to-all-done.q_ref = bf16[4,128,512]{2,1,0:T(8,128)(2,1)S(1)} async-done(((bf16[4,128,512]{2,1,0:T(8,128)(2,1)}), bf16[4,128,512]{2,1,0:T(8,128)(2,1)S(1)}, u32[]{:S(2)}, u32[]{:S(2)}) %all-to-all-start) | async-done | bytes 524320 | tf_op jit(solution)/shard_map/all_to_all | solution.py:175
  34.2 3.5 %all-to-all-start.1 = ((bf16[4,128,512]{2,1,0:T(8,128)(2,1)}), bf16[4,128,512]{2,1,0:T(8,128)(2,1)S(1)}, u32[]{:S(2)}, u32[]{:S(2)}) async-start(bf16[4,128,512]{2,1,0:T(8,128)(2,1)} %bitcast.4), calls=%async_computation.1 | async-start | bytes 1048576 | tf_op jit(solution)/shard_map/all_to_all | solution.py:176
  37.7 0.0 reduce-scatter.2.cloned.1.call-start
  37.8 8.0 %all-to-all-done.1.do_ref = bf16[4,128,512]{2,1,0:T(8,128)(2,1)S(1)} async-done(((bf16[4,128,512]{2,1,0:T(8,128)(2,1)}), bf16[4,128,512]{2,1,0:T(8,128)(2,1)S(1)}, u32[]{:S(2)}, u32[]{:S(2)}) %all-to-all-start.1) | async-done | bytes 524320 | tf_op jit(solution)/shard_map/all_to_all | solution.py:176
  45.8 17.5 %all-gather.2.cloned.1.call-done.kv_ref = bf16[32,128,256]{2,1,0:T(8,128)(2,1)} async-done(((bf16[4,128,256]{2,1,0:T(8,128)(2,1)}), bf16[32,128,256]{2,1,0:T(8,128)(2,1)}) %all-gather.2.cloned.1.call-update) | async-done | bytes 2097168 | tf_op jit(solution)/shard_map/all_gather | solution.py:174
  63.3 0.0 copy-done
  63.3 0.0 copy-done.1
  63.3 15.0 %attention.1 = (bf16[4,128,512]{2,1,0:T(8,128)(2,1)S(1)}, bf16[4,128,512]{2,1,0:T(8,128)(2,1)S(1)}, bf16[32,128,256]{2,1,0:T(8,128)(2,1)}) custom-call(s32[32]{0:T(128)S(1)} %copy-done, s32[4]{0:T(128)S(1)} %copy-done.1, s32[1]{0:T(128)} %bitcast.z_ref, bf16[4,128,512]{2,1,0:T(8,128)(2,1)S(1)} %all-to-all-done.q_ref, ...), custom_call_target="tpu_custom_call" | custom-call | tf_op jit(solution)/shard_map/attention/pallas_call | solution.py:148
  78.3 0.0 reduce-scatter.2.cloned.1.call-update
  78.3 14.5 %all_to_all.31 = bf16[4,128,512]{2,1,0:T(8,128)(2,1)S(1)} all-to-all(bf16[4,128,512]{2,1,0:T(8,128)(2,1)S(1)} %get-tuple-element.7), channel_id=1, replica_groups=mesh['dp'=8,'x'=4,'z'=8] {'x'}, dimensions={0} | all-to-all | bytes 1048576 | tf_op jit(solution)/shard_map/all_to_all | solution.py:180
  92.8 11.8 %all_to_all.32 = bf16[4,128,512]{2,1,0:T(8,128)(2,1)S(1)} all-to-all(bf16[4,128,512]{2,1,0:T(8,128)(2,1)S(1)} %get-tuple-element.8), channel_id=1, replica_groups=mesh['dp'=8,'x'=4,'z'=8] {'x'}, dimensions={0} | all-to-all | bytes 1048576 | tf_op jit(solution)/shard_map/all_to_all | solution.py:181
  104.6 29.8 %reduce-scatter.2.cloned.1.call-done = bf16[4,128,256]{2,1,0:T(8,128)(2,1)} async-done(((bf16[32,128,256]{2,1,0:T(8,128)(2,1)}), bf16[4,128,256]{2,1,0:T(8,128)(2,1)}) %reduce-scatter.2.cloned.1.call-update) | async-done | bytes 262160 | tf_op jit(solution)/shard_map/reduce_scatter | solution.py:178
  134.4 4.3 %all-to-all-start.5 = ((bf16[4,128,256]{2,1,0:T(8,128)(2,1)}), bf16[4,128,256]{2,1,0:T(8,128)(2,1)S(1)}, u32[]{:S(2)}, u32[]{:S(2)}) async-start(bf16[4,128,256]{2,1,0:T(8,128)(2,1)} %reduce-scatter.2.cloned.1.call-done), calls=%async_computation.6 | async-start | bytes 524288 | tf_op jit(solution)/shard_map/all_to_all | solution.py:179
  138.6 0.3 copy.33
  138.9 1.0 copy.37
  139.9 0.3 copy.34
  140.2 1.0 copy.38
  141.2 4.1 %all-to-all-done.5 = bf16[4,128,256]{2,1,0:T(8,128)(2,1)S(1)} async-done(((bf16[4,128,256]{2,1,0:T(8,128)(2,1)}), bf16[4,128,256]{2,1,0:T(8,128)(2,1)S(1)}, u32[]{:S(2)}, u32[]{:S(2)}) %all-to-all-start.5) | async-done | bytes 262176 | tf_op jit(solution)/shard_map/all_to_all | solution.py:179
  145.4 0.1 copy.36
  145.5 0.8 copy.40
  146.3 0.1 copy.35
  146.4 0.8 copy.39
  (2 shorter events, 0.1 us)
Async XLA Ops:
  7.2 13.8 %copy-start.2 = (bf16[128,2048]{1,0:T(8,128)(2,1)S(1)}, bf16[128,2048]{1,0:T(8,128)(2,1)}, u32[]{:S(2)}) copy-start(bf16[128,2048]{1,0:T(8,128)(2,1)} %param.6) | copy-start | bytes 1572868
  7.2 56.1 %all-gather.2.cloned.1.call-start = ((), (), s32[]{:S(2)}) async-start(), calls=%async_computation.7 | async-start | bytes 2359296 | tf_op jit(solution)/shard_map/all_gather | solution.py:174
  20.1 5.8 %copy-start.3 = (bf16[128,2048]{1,0:T(8,128)(2,1)S(1)}, bf16[128,2048]{1,0:T(8,128)(2,1)}, u32[]{:S(2)}) copy-start(bf16[128,2048]{1,0:T(8,128)(2,1)} %param.9) | copy-start | bytes 1572868
  22.3 41.0 %copy-start = (s32[32]{0:T(128)S(1)}, s32[32]{0:T(128)}, u32[]{:S(2)}) copy-start(s32[32]{0:T(128)} %span_ref.1) | copy-start | bytes 388
  22.3 41.0 %copy-start.1 = (s32[4]{0:T(128)S(1)}, s32[4]{0:T(128)}, u32[]{:S(2)}) copy-start(s32[4]{0:T(128)} %doc_ref.1) | copy-start | bytes 52
  22.3 11.9 %all-to-all-start = ((bf16[4,128,512]{2,1,0:T(8,128)(2,1)}), bf16[4,128,512]{2,1,0:T(8,128)(2,1)S(1)}, u32[]{:S(2)}, u32[]{:S(2)}) async-start(bf16[4,128,512]{2,1,0:T(8,128)(2,1)} %bitcast.2), calls=%async_computation | async-start | bytes 1048576 | tf_op jit(solution)/shard_map/all_to_all | solution.py:175
  34.2 11.5 %all-to-all-start.1 = ((bf16[4,128,512]{2,1,0:T(8,128)(2,1)}), bf16[4,128,512]{2,1,0:T(8,128)(2,1)S(1)}, u32[]{:S(2)}, u32[]{:S(2)}) async-start(bf16[4,128,512]{2,1,0:T(8,128)(2,1)} %bitcast.4), calls=%async_computation.1 | async-start | bytes 1048576 | tf_op jit(solution)/shard_map/all_to_all | solution.py:176
  37.7 96.6 %reduce-scatter.2.cloned.1.call-start = ((), (), s32[]{:S(2)}) async-start(), calls=%async_computation.8 | async-start | bytes 2359296 | tf_op jit(solution)/shard_map/reduce_scatter | solution.py:178
  134.4 11.0 %all-to-all-start.5 = ((bf16[4,128,256]{2,1,0:T(8,128)(2,1)}), bf16[4,128,256]{2,1,0:T(8,128)(2,1)S(1)}, u32[]{:S(2)}, u32[]{:S(2)}) async-start(bf16[4,128,256]{2,1,0:T(8,128)(2,1)} %reduce-scatter.2.cloned.1.call-done), calls=%async_computation.6 | async-start | bytes 524288 | tf_op jit(solution)/shard_map/all_to_all | solution.py:179
Sparse Core Ops, SparseCore 0:
  21.1 42.1 all-gather.1
  78.4 55.8 reduce-scatter.1

commit v2 on v1

v2 whole, which is shorter than its diff:
```python
import functools

import jax
import jax.numpy as jnp
from jax import lax
from jax.experimental import pallas as pl
from jax.experimental.pallas import tpu as pltpu
from jax.sharding import Mesh, PartitionSpec as P

HEADS = 4
D = 128
B = 128
NX, NH, NL = 4, 4, 2
W = HEADS * B
SEEN = 18
STEP = 4
STEPS = -(-SEEN // STEP)
SCALE = D ** -0.5
SCALE_LOG2 = SCALE * 1.4426950408889634
FILL = -1e30
BF, F32 = jnp.bfloat16, jnp.float32
VM = pl.BlockSpec(memory_space=pltpu.VMEM)
SM = pl.BlockSpec(memory_space=pltpu.SMEM)
ROOM = pltpu.CompilerParams(vmem_limit_bytes=48 * 2 ** 20)


def nt(a, b):
    return lax.dot_general(a, b, (((1,), (1,)), ((), ())), preferred_element_type=F32)


def tn(a, b):
    return lax.dot_general(a, b, (((0,), (0,)), ((), ())), preferred_element_type=F32)


def nn(a, b):
    return lax.dot_general(a, b, (((1,), (0,)), ((), ())), preferred_element_type=F32)


def sds(*shape, dtype=BF):
    return jax.ShapeDtypeStruct(shape, dtype)


class Places:
    def __init__(self, fact_ref, me_ref, shifts, table_ref, list_ref):
        self.fact_ref, self.me_ref = fact_ref, me_ref
        self.table_ref, self.list_ref = table_ref, list_ref
        self.count = 2 * NH * len(shifts)
        self.ends = []
        total = jnp.int32(0)
        for i in range(4):
            total = total + fact_ref[NX * NH * NL + i]
            self.ends.append(total)
        for side in range(2):
            for k, dx in enumerate(shifts):
                for step in range(NH):
                    index = (side * len(shifts) + k) * NH + step
                    table_ref[index] = self.span(dx, step, side)

    def span(self, dx, step, side):
        e, x, zh = self.me_ref[0], self.me_ref[1], self.me_ref[2]
        from_x = lax.rem(x + NX - dx, NX)
        from_zh = lax.rem(zh + NH - step, NH)
        return self.fact_ref[(from_x * NH + from_zh) * NL + lax.rem(e + side, NL)]

    def of_query_block(self, i):
        span = self.span(0, i, 0)
        first = span * B
        self.q_pos = first + lax.rem(lax.broadcasted_iota(jnp.int32, (1, W), 1), B)
        self.q_start = jnp.zeros((1, W), jnp.int32)
        start_first = jnp.int32(0)
        for e in self.ends:
            start_first = jnp.where(e <= first, e, start_first)
            self.q_start = jnp.where(e <= self.q_pos, e, self.q_start)
        low = start_first // B
        n = jnp.int32(0)
        for j in range(self.count):
            s = self.table_ref[j]
            self.list_ref[n] = j
            n = n + jnp.where((s >= low) & (s <= span), 1, 0)
        for j in range(STEP - 1):
            self.list_ref[n + j] = 0
        self.n = n
        return (n + STEP - 1) // STEP

    def blocks(self, c):
        return [self.list_ref[STEP * c + j] for j in range(STEP)]

    def mask(self, c, blocks):
        row = lax.broadcasted_iota(jnp.int32, (B, W), 0)
        parts = []
        for j, block in enumerate(blocks):
            first = jnp.where(STEP * c + j < self.n, self.table_ref[block] * B, SEEN * B * 4)
            k_pos = row + first
            parts.append((k_pos >= self.q_start) & (k_pos <= self.q_pos))
        return jnp.concatenate(parts, axis=0)


def stacked(ref, i):
    return jnp.concatenate([ref[i, :, h * D:(h + 1) * D] for h in range(HEADS)], axis=0)


def taken(ref, blocks, cols):
    return jnp.concatenate([ref[block, :, cols] for block in blocks], axis=0)


SHIFTS = (0, 1, 2, 3)
KEYS, VALUES = slice(0, D), slice(D, 2 * D)


def forward_kernel(fact_ref, me_ref, q_ref, do_ref, own_ref, sib_ref, o_ref, stat_ref,
                   s_ref, kv_ref, table_ref, list_ref):
    half = NX * NH
    kv_ref[:half] = own_ref[...]
    kv_ref[half:] = sib_ref[...]
    places = Places(fact_ref, me_ref, SHIFTS, table_ref, list_ref)

    def one_block(i, carry):
        steps = places.of_query_block(i)
        qs = stacked(q_ref, i)

        def score_step(c, m):
            blocks = places.blocks(c)
            st = nt(taken(kv_ref, blocks, KEYS), qs) * SCALE_LOG2
            st = jnp.where(places.mask(c, blocks), st, FILL)
            s_ref[c] = st
            return jnp.maximum(m, jnp.max(st.reshape(-1, 8, W), axis=0))

        m = lax.fori_loop(0, steps, score_step, jnp.full((8, W), FILL, F32))
        m = jnp.max(m, axis=0, keepdims=True)

        def weigh_step(c, state):
            l, ot = state
            blocks = places.blocks(c)
            p = jnp.exp2(s_ref[c] - m)
            return (
                l + jnp.sum(p.reshape(-1, 8, W), axis=0),
                ot + tn(taken(kv_ref, blocks, VALUES), p.astype(BF)),
            )

        state = jnp.zeros((8, W), F32), jnp.zeros((D, W), F32)
        l, ot = lax.fori_loop(0, steps, weigh_step, state)
        l = jnp.sum(l, axis=0, keepdims=True)
        ob = (ot * (1.0 / l)).astype(BF)
        delta = []
        for h in range(HEADS):
            cols = slice(h * B, (h + 1) * B)
            of = ob[:, cols].astype(F32)
            o_ref[i, :, cols] = of.T.astype(BF)
            dot = do_ref[i, :, cols].astype(F32).T
            delta.append(jnp.sum(of * dot, axis=0, keepdims=True))
        stat_ref[i, 0:1, :] = m + jnp.log2(l)
        stat_ref[i, 1:2, :] = jnp.concatenate(delta, axis=1)
        return carry

    lax.fori_loop(0, NH, one_block, 0)


def forward(facts, me, q, do, own, sib):
    blocks = 2 * NX * NH
    return pl.pallas_call(
        forward_kernel,
        in_specs=[SM] * 2 + [VM] * 4,
        out_specs=[VM] * 2,
        out_shape=[sds(NH, B, W), sds(NH, 8, W, dtype=F32)],
        scratch_shapes=[
            pltpu.VMEM((STEPS, STEP * B, W), F32),
            pltpu.VMEM((blocks, B, 2 * D), BF),
            pltpu.SMEM((blocks,), jnp.int32),
            pltpu.SMEM((blocks + 8,), jnp.int32),
        ],
        compiler_params=ROOM,
        cost_estimate=pl.CostEstimate(flops=8 * 10 ** 9, bytes_accessed=4 * 10 ** 6, transcendentals=0),
        name="forward",
    )(facts, me, q, do, own, sib)


def backward_kernel(shifts, first, last, *refs):
    refs = list(refs)
    n = len(shifts)
    fact_ref, me_ref, q_ref, do_ref, stat_ref = refs[:5]
    chunks, rest = refs[5:5 + 2 * n], refs[5 + 2 * n:]
    if not first:
        dqt_in = rest[0]
        rest = rest[1:]
    if last:
        o_ref = rest[0]
        rest = rest[1:]
    own_out, sib_out, dq_out, s_ref, acc_ref, kv_ref, table_ref, list_ref = rest
    for k, ref in enumerate(chunks):
        kv_ref[k * NH:(k + 1) * NH] = ref[...]
    places = Places(fact_ref, me_ref, shifts, table_ref, list_ref)
    acc_ref[...] = jnp.zeros_like(acc_ref)

    def one_block(i, carry):
        steps = places.of_query_block(i)
        qs, dos = stacked(q_ref, i), stacked(do_ref, i)
        lse, delta = stat_ref[i, 0:1, :], stat_ref[i, 1:2, :]

        def step(c, dqt):
            blocks = places.blocks(c)
            keys = taken(kv_ref, blocks, KEYS)
            st = nt(keys, qs) * SCALE_LOG2 - lse
            p = jnp.exp2(jnp.where(places.mask(c, blocks), st, FILL))
            dp = nt(taken(kv_ref, blocks, VALUES), dos)
            ds = (p * (dp - delta)).astype(BF)
            dv = nn(p.astype(BF), dos)
            dk = nn(ds, qs)
            for j, block in enumerate(blocks):
                acc_ref[block, :, KEYS] += dk[j * B:(j + 1) * B]
                acc_ref[block, :, VALUES] += dv[j * B:(j + 1) * B]
            return dqt + tn(keys, ds)

        dqt = lax.fori_loop(0, steps, step, jnp.zeros((D, W), F32) if first else dqt_in[i])
        if last:
            dq_out[i, :, :W] = o_ref[i]
            for h in range(HEADS):
                cols = slice(h * B, (h + 1) * B)
                dq_out[i, :, W + h * B:W + (h + 1) * B] = (dqt[:, cols] * SCALE).T.astype(BF)
        else:
            dq_out[i] = dqt
        return carry

    lax.fori_loop(0, NH, one_block, 0)
    for side, ref in enumerate((own_out, sib_out)):
        for j in range(n * NH):
            at = side * n * NH + j
            ref[j, :, KEYS] = (acc_ref[at, :, KEYS] * SCALE).astype(BF)
            ref[j, :, VALUES] = acc_ref[at, :, VALUES].astype(BF)


def backward(shifts, facts, me, q, do, stat, own, sib, dqt, o):
    first, last = dqt is None, o is not None
    n = len(shifts)
    tail = ([] if first else [dqt]) + ([o] if last else [])
    args = [facts, me, q, do, stat] + [own] * n + [sib] * n + tail
    chunk_specs = [
        pl.BlockSpec((NH, B, 2 * D), lambda g, k=SHIFTS.index(dx): (k, 0, 0)) for dx in shifts
    ]
    dq = sds(NH, B, 2 * W) if last else sds(NH, D, W, dtype=F32)
    return pl.pallas_call(
        functools.partial(backward_kernel, shifts, first, last),
        grid=(1,),
        in_specs=[SM] * 2 + [VM] * 3 + chunk_specs * 2 + [VM] * len(tail),
        out_specs=[VM] * 3,
        out_shape=[sds(n * NH, B, 2 * D)] * 2 + [dq],
        scratch_shapes=[
            pltpu.VMEM((STEP * B, W), F32),
            pltpu.VMEM((2 * n * NH, B, 2 * D), F32),
            pltpu.VMEM((2 * n * NH, B, 2 * D), BF),
            pltpu.SMEM((2 * n * NH,), jnp.int32),
            pltpu.SMEM((2 * n * NH + 8,), jnp.int32),
        ],
        compiler_params=ROOM,
        cost_estimate=pl.CostEstimate(
            flops=5 * n * 10 ** 9, bytes_accessed=4 * 10 ** 6, transcendentals=0
        ),
        name="backward",
    )(*args)


def pack_kernel(me_ref, *refs):
    arrays, outs = refs[:-NH], refs[-NH:]
    for s, out in enumerate(outs):
        group, at = lax.rem(me_ref[2] + s, NH), 0
        for ref in arrays:
            width = ref.shape[1] // NH
            out[:, at:at + width] = ref[:, pl.ds(pl.multiple_of(group * width, width), width)]
            at += width


def pack(me, *arrays):
    width = sum(a.shape[1] for a in arrays) // NH
    return pl.pallas_call(
        pack_kernel,
        in_specs=[SM] + [VM] * len(arrays),
        out_specs=[VM] * NH,
        out_shape=[sds(B, width)] * NH,
        name="pack",
    )(me, *arrays)


def unpack_kernel(me_ref, *refs):
    odq, dkv, outs = refs[:NH], refs[NH:2 * NH], refs[2 * NH:]
    for s in range(NH):
        group = lax.rem(me_ref[2] + s, NH)
        for piece, pair in ((odq[s], outs[:2]), (dkv[s], outs[2:])):
            width = piece.shape[1] // 2
            cols = pl.ds(pl.multiple_of(group * width, width), width)
            for k, out in enumerate(pair):
                out[:, cols] = piece[:, k * width:(k + 1) * width]


def unpack(me, odq, dkv):
    return pl.pallas_call(
        unpack_kernel,
        in_specs=[SM] + [VM] * (2 * NH),
        out_specs=[VM] * 4,
        out_shape=[sds(B, NH * W)] * 2 + [sds(B, NH * D)] * 2,
        name="unpack",
    )(me, *odq, *dkv)


def by_heads(pieces, sign):
    out = []
    for s in range(NH):
        perm = [
            ((c * NH + h) * NL + l, (l * NH + (h + sign * s) % NH) * NL + c)
            for c in range(2) for h in range(NH) for l in range(NL)
        ]
        out.append(lax.ppermute(pieces[s], ("core", "zh", "zl"), perm))
    return out


def to_x(array, shift):
    return lax.ppermute(array, "x", [(i, (i + shift) % NX) for i in range(NX)])


def to_sibling(array):
    return lax.ppermute(array, "core", [(0, 1), (1, 0)])


def on_device(queries, key_vectors, value_vectors, output_cotangent, doc_lengths, span_of):
    core, zl = lax.axis_index("core"), lax.axis_index("zl")
    me = jnp.stack([core, lax.axis_index("x"), lax.axis_index("zh")]).astype(jnp.int32)
    kvq = jnp.stack(by_heads(pack(me, key_vectors, value_vectors, queries), 1))
    kv, q = kvq[:, :, :2 * D], kvq[:, :, 2 * D:]
    do_pieces = pack(me, output_cotangent)
    do = jnp.stack(by_heads(do_pieces, 1))
    facts = jnp.concatenate([span_of, doc_lengths])
    facts = jnp.where(core == zl, facts, to_sibling(facts))
    own = jnp.concatenate([kv] + [to_x(kv, dx) for dx in SHIFTS[1:]])
    own, do, facts = lax.optimization_barrier((own, do, facts))
    sib = to_sibling(own)
    o, stat = forward(facts, me, q, do, own, sib)
    args = facts, me, q, do, stat, own, sib
    mine2, theirs2, dqt = backward((2,), *args, None, None)
    mine13, theirs13, dqt = backward((1, 3), *args, dqt, None)
    mine0, theirs0, odq = backward((0,), *args, dqt, o)

    def added(mine, theirs):
        return mine.astype(F32) + to_sibling(theirs).astype(F32)

    sum2, sum13 = added(mine2, theirs2).astype(BF), added(mine13, theirs13).astype(BF)
    total = added(mine0, theirs0)
    for array, dx in ((sum2, 2), (sum13[:NH], 1), (sum13[NH:], 3)):
        total = total + to_x(array, -dx).astype(F32)
    total = total.astype(BF)
    dkv = by_heads([total[s] for s in range(NH)], -1)
    odq = by_heads([odq[s] for s in range(NH)], -1)
    return unpack(me, odq, dkv)


def solution(mesh):
    split = Mesh(
        mesh.devices.reshape(-1, 2, NX, NH, NL), ("y", "core", "x", "zh", "zl")
    )
    rows = P(("y", "core", "x", "zh", "zl"), None)
    part = P(("y", "core"))
    return jax.shard_map(
        on_device,
        mesh=split,
        in_specs=(rows, rows, rows, rows, part, part),
        out_specs=(rows, rows, rows, rows),
        check_vma=False,
    )
```

time: 154 us -> 141 us (0.916)
  the two profiles are of different devices: /device:TPU:8 before, /device:TPU:17 now
where the time goes in v2:
time: 141 us; the launch traced here: 140 us
  starting transfers between devices  62.2 us (44%)
  waiting for transfers between devices  36.6 us (26%)
  Pallas kernels  35.9 us (25%)
  local copies, waits for them, and re-layouts  3.33 us (2%)
  other arithmetic  1.41 us (1%)
    ppermute x16, starting transfers between devices, by_heads(): out.append(lax.ppermute(pieces[s], ('core', 'zh', 'zl'), perm))  50.4 us
    pallas_call x3, Pallas kernels, backward(): pl.pallas_call(functools.partial(backward_kernel, shifts, first, last), g...  19.7 us
    ppermute x16, waiting for transfers between devices, by_heads(): out.append(lax.ppermute(pieces[s], ('core', 'zh', 'zl'), perm))  18.5 us
    ppermute x6, waiting for transfers between devices, to_x(): return lax.ppermute(array, 'x', [(i, (i + shift) % NX) for i in range(NX)])  14.7 us
    pallas_call x1, Pallas kernels, forward(): pl.pallas_call(forward_kernel, in_specs=[SM] * 2 + [VM] * 4, out_specs=[V...  9.79 us
    ppermute x6, starting transfers between devices, to_x(): return lax.ppermute(array, 'x', [(i, (i + shift) % NX) for i in range(NX)])  6.44 us
    ppermute x5, starting transfers between devices, to_sibling(): return lax.ppermute(array, 'core', [(0, 1), (1, 0)])  5.3 us
    pallas_call x2, Pallas kernels, pack(): pl.pallas_call(pack_kernel, in_specs=[SM] + [VM] * len(arrays), out_specs...  4.03 us
  transfers between devices with their start and end apart: 27, of which 13 were waited for; matrix products, arithmetic and copies ran while one was open for 1% of the time, Pallas kernels for 12%

profile of v2, /device:TPU:17, one launch (start us, length us, event | category | flops | bytes accessed | tf_op | source)
XLA Modules:
  0.0 140.3 jit_solution(10194377943332331755)
XLA Ops:
  0.6 0.6 pad_add_fusion.me_ref.refs_1_
  1.3 2.1 %pack.2 = (bf16[128,768]{1,0:T(8,128)(2,1)}, bf16[128,768]{1,0:T(8,128)(2,1)}, bf16[128,768]{1,0:T(8,128)(2,1)}, bf16[128,768]{1,0:T(8,128)(2,1)}) custom-call(s32[3]{0:T(128)} %pad_add_fusion.me_ref.refs_1_, bf16[128,512]{1,0:T(8,128)(2,1)} %refs_0_.2, bf16[128,512]{1,0:T(8,128)(2,1)} %refs_1_.1, bf16[128,2048]{1,0:T(8,128)(2,1)} %refs_2_.1), custom_call_target="tpu_custom_call" | custom-call | tf_op jit(solution)/shard_map/pack/pallas_call | solution.py:273
  3.4 4.1 %collective-permute-start = (bf16[128,768]{1,0:T(8,128)(2,1)}, bf16[128,768]{1,0:T(8,128)(2,1)S(1)}, u32[]{:S(2)}, u32[]{:S(2)}) collective-permute-start(bf16[128,768]{1,0:T(8,128)(2,1)} %get-tuple-element.26), channel_id=1, source_target_pairs={{0,0},{1,32},{2,2},{3,34},{4,4},{5,36},{6,6},{7,38},{32,1},{33,33}... | collective-permute-start | bytes 589832 | tf_op jit(solution)/shard_map/ppermute | solution.py:310
  7.5 2.8 %collective-permute-start.1 = (bf16[128,768]{1,0:T(8,128)(2,1)}, bf16[128,768]{1,0:T(8,128)(2,1)S(1)}, u32[]{:S(2)}, u32[]{:S(2)}) collective-permute-start(bf16[128,768]{1,0:T(8,128)(2,1)} %get-tuple-element.27), channel_id=1, source_target_pairs={{0,2},{1,34},{2,4},{3,36},{4,6},{5,38},{6,0},{7,32},{32,3},{33,35}... | collective-permute-start | bytes 589832 | tf_op jit(solution)/shard_map/ppermute | solution.py:310
  10.3 3.9 %collective-permute-start.2 = (bf16[128,768]{1,0:T(8,128)(2,1)}, bf16[128,768]{1,0:T(8,128)(2,1)S(1)}, u32[]{:S(2)}, u32[]{:S(2)}) collective-permute-start(bf16[128,768]{1,0:T(8,128)(2,1)} %get-tuple-element.28), channel_id=1, source_target_pairs={{0,4},{1,36},{2,6},{3,38},{4,0},{5,32},{6,2},{7,34},{32,5},{33,37}... | collective-permute-start | bytes 589832 | tf_op jit(solution)/shard_map/ppermute | solution.py:310
  14.2 2.5 %collective-permute-start.3 = (bf16[128,768]{1,0:T(8,128)(2,1)}, bf16[128,768]{1,0:T(8,128)(2,1)S(1)}, u32[]{:S(2)}, u32[]{:S(2)}) collective-permute-start(bf16[128,768]{1,0:T(8,128)(2,1)} %get-tuple-element.29), channel_id=1, source_target_pairs={{0,6},{1,38},{2,0},{3,32},{4,2},{5,34},{6,4},{7,36},{32,7},{33,39}... | collective-permute-start | bytes 589832 | tf_op jit(solution)/shard_map/ppermute | solution.py:310
  16.7 1.9 %pack.3 = (bf16[128,512]{1,0:T(8,128)(2,1)}, bf16[128,512]{1,0:T(8,128)(2,1)}, bf16[128,512]{1,0:T(8,128)(2,1)}, bf16[128,512]{1,0:T(8,128)(2,1)}) custom-call(s32[3]{0:T(128)} %pad_add_fusion.me_ref.refs_1_, bf16[128,2048]{1,0:T(8,128)(2,1)} %refs_0_.3), custom_call_target="tpu_custom_call" | custom-call | tf_op jit(solution)/shard_map/pack/pallas_call | solution.py:273
  18.6 0.0 collective-permute-start.10
  18.7 3.2 %collective-permute-start.7 = (bf16[128,512]{1,0:T(8,128)(2,1)}, bf16[128,512]{1,0:T(8,128)(2,1)S(1)}, u32[]{:S(2)}, u32[]{:S(2)}) collective-permute-start(bf16[128,512]{1,0:T(8,128)(2,1)} %get-tuple-element.30), channel_id=1, source_target_pairs={{0,0},{1,32},{2,2},{3,34},{4,4},{5,36},{6,6},{7,38},{32,1},{33,33}... | collective-permute-start | bytes 393224 | tf_op jit(solution)/shard_map/ppermute | solution.py:310
  21.9 0.1 pad_add_fusion.1
  22.0 0.0 collective-permute-done.1
  22.0 2.6 %collective-permute-start.8 = (bf16[128,512]{1,0:T(8,128)(2,1)}, bf16[128,512]{1,0:T(8,128)(2,1)S(1)}, u32[]{:S(2)}, u32[]{:S(2)}) collective-permute-start(bf16[128,512]{1,0:T(8,128)(2,1)} %get-tuple-element.31), channel_id=1, source_target_pairs={{0,2},{1,34},{2,4},{3,36},{4,6},{5,38},{6,0},{7,32},{32,3},{33,35}... | collective-permute-start | bytes 393224 | tf_op jit(solution)/shard_map/ppermute | solution.py:310
  24.6 4.7 %collective-permute-done.2 = bf16[128,768]{1,0:T(8,128)(2,1)S(1)} collective-permute-done((bf16[128,768]{1,0:T(8,128)(2,1)}, bf16[128,768]{1,0:T(8,128)(2,1)S(1)}, u32[]{:S(2)}, u32[]{:S(2)}) %collective-permute-start.2) | collective-permute-done | bytes 196640 | tf_op jit(solution)/shard_map/ppermute | solution.py:310
  29.3 4.3 %collective-permute-start.9 = (bf16[128,512]{1,0:T(8,128)(2,1)}, bf16[128,512]{1,0:T(8,128)(2,1)S(1)}, u32[]{:S(2)}, u32[]{:S(2)}) collective-permute-start(bf16[128,512]{1,0:T(8,128)(2,1)} %get-tuple-element.32), channel_id=1, source_target_pairs={{0,4},{1,36},{2,6},{3,38},{4,0},{5,32},{6,2},{7,34},{32,5},{33,37}... | collective-permute-start | bytes 393224 | tf_op jit(solution)/shard_map/ppermute | solution.py:310
  33.5 4.3 %collective-permute-done.3 = bf16[128,768]{1,0:T(8,128)(2,1)S(1)} collective-permute-done((bf16[128,768]{1,0:T(8,128)(2,1)}, bf16[128,768]{1,0:T(8,128)(2,1)S(1)}, u32[]{:S(2)}, u32[]{:S(2)}) %collective-permute-start.3) | collective-permute-done | bytes 196640 | tf_op jit(solution)/shard_map/ppermute | solution.py:310
  37.8 0.0 collective-permute-start.11
  37.9 1.1 collective-permute-done.11
  39.0 1.2 collective-permute-start.4
  40.2 2.5 %collective-permute-start.5 = (bf16[4,128,256]{2,1,0:T(8,128)(2,1)S(1)}, bf16[4,128,256]{2,1,0:T(8,128)(2,1)S(1)}, u32[]{:S(2)}, u32[]{:S(2)}) collective-permute-start(bf16[4,128,256]{2,1,0:T(8,128)(2,1)S(1)} %pad_maximum_fusion.5), channel_id=1, source_target_pairs={{0,16},{8,24},{16,0},{24,8},{1,17},{9,25},{17,1},{25,9},{2,18},{10... | collective-permute-start | bytes 786440 | tf_op jit(solution)/shard_map/ppermute | solution.py:315
  42.6 0.0 collective-permute-done.7
  42.6 1.2 collective-permute-start.6
  43.8 0.1 broadcast_select_fusion.fact_ref.refs_0_
  43.9 0.0 collective-permute-done.8
  43.9 0.0 collective-permute-done.9
  43.9 0.1 pad_maximum_fusion.4.do_ref.refs_3_
  43.9 3.9 %collective-permute-done.4 = bf16[4,128,256]{2,1,0:T(8,128)(2,1)S(1)} collective-permute-done((bf16[4,128,256]{2,1,0:T(8,128)(2,1)S(1)}, bf16[4,128,256]{2,1,0:T(8,128)(2,1)S(1)}, u32[]{:S(2)}, u32[]{:S(2)}) %collective-permute-start.4) | collective-permute-done | bytes 262176 | tf_op jit(solution)/shard_map/ppermute | solution.py:315
  47.9 6.6 %collective-permute-done.5 = bf16[4,128,256]{2,1,0:T(8,128)(2,1)S(1)} collective-permute-done((bf16[4,128,256]{2,1,0:T(8,128)(2,1)S(1)}, bf16[4,128,256]{2,1,0:T(8,128)(2,1)S(1)}, u32[]{:S(2)}, u32[]{:S(2)}) %collective-permute-start.5) | collective-permute-done | bytes 262176 | tf_op jit(solution)/shard_map/ppermute | solution.py:315
  54.5 0.6 collective-permute-done.6
  55.1 0.1 pad_maximum_fusion.own_ref.refs_5_.refs_6_
  55.2 0.8 collective-permute-start.12
  56.0 2.2 %collective-permute-done.12.sib_ref.refs_6_.refs_7_.refs_8_ = bf16[16,128,256]{2,1,0:T(8,128)(2,1)S(1)} collective-permute-done((bf16[16,128,256]{2,1,0:T(8,128)(2,1)S(1)}, bf16[16,128,256]{2,1,0:T(8,128)(2,1)S(1)}, u32[]{:S(2)}, u32[]{:S(2)}) %collective-permute-start.12) | collective-permute-done | bytes 1048608 | tf_op jit(solution)/shard_map/ppermute | solution.py:319
  58.3 9.8 %forward.1 = (bf16[4,128,512]{2,1,0:T(8,128)(2,1)S(1)}, f32[4,8,512]{2,1,0:T(8,128)S(1)}) custom-call(s32[36]{0:T(128)S(1)} %broadcast_select_fusion.fact_ref.refs_0_, s32[3]{0:T(128)S(1)} %copy-done, bf16[4,128,512]{2,1,0:T(8,128)(2,1)S(1)} %pad_maximum_fusion.1.q_ref.refs_2_, bf16[4,128,512]{2,1,0:T(8,128)(2,1)S(1)} %pad_maximum_fusion.4.do_ref.refs_3_, ...), custom_call_target="tpu_custom_call" | custom-call | flops 8000000000 | bytes 4000000 | tf_op jit(solution)/shard_map/forward/pallas_call | solution.py:160
  68.1 4.9 %backward.3 = (bf16[4,128,256]{2,1,0:T(8,128)(2,1)S(1)}, bf16[4,128,256]{2,1,0:T(8,128)(2,1)S(1)}, f32[4,128,512]{2,1,0:T(8,128)S(1)}) custom-call(s32[36]{0:T(128)S(1)} %broadcast_select_fusion.fact_ref.refs_0_, s32[3]{0:T(128)S(1)} %copy-done, bf16[4,128,512]{2,1,0:T(8,128)(2,1)S(1)} %pad_maximum_fusion.1.q_ref.refs_2_, ...), custom_call_target="tpu_custom_call" | custom-call | flops 5000000000 | bytes 4000000 | tf_op jit(solution)/shard_map/backward/pallas_call | solution.py:240
  73.0 1.0 copy-done.2
  74.0 2.5 %collective-permute-start.18 = (bf16[4,128,256]{2,1,0:T(8,128)(2,1)S(1)}, bf16[4,128,256]{2,1,0:T(8,128)(2,1)S(1)}, u32[]{:S(2)}, u32[]{:S(2)}) collective-permute-start(bf16[4,128,256]{2,1,0:T(8,128)(2,1)S(1)} %get-tuple-element.45), channel_id=1, source_target_pairs={{0,32},{32,0},{1,33},{33,1},{2,34},{34,2},{3,35},{35,3},{4,36},{36... | collective-permute-start | bytes 786440 | tf_op jit(solution)/shard_map/ppermute | solution.py:319
  76.5 7.9 %backward.4 = (bf16[8,128,256]{2,1,0:T(8,128)(2,1)S(1)}, bf16[8,128,256]{2,1,0:T(8,128)(2,1)S(1)}, f32[4,128,512]{2,1,0:T(8,128)S(1)}) custom-call(s32[36]{0:T(128)S(1)} %broadcast_select_fusion.fact_ref.refs_0_, s32[3]{0:T(128)S(1)} %copy-done, bf16[4,128,512]{2,1,0:T(8,128)(2,1)S(1)} %pad_maximum_fusion.1.q_ref.refs_2_, ...), custom_call_target="tpu_custom_call" | custom-call | flops 10000000000 | bytes 4000000 | tf_op jit(solution)/shard_map/backward/pallas_call | solution.py:240
  84.4 1.0 copy-done.1
  85.4 1.0 collective-permute-start.20
  86.3 6.9 %backward.5 = (bf16[4,128,256]{2,1,0:T(8,128)(2,1)S(1)}, bf16[4,128,256]{2,1,0:T(8,128)(2,1)S(1)}, bf16[4,128,1024]{2,1,0:T(8,128)(2,1)S(1)}) custom-call(s32[36]{0:T(128)S(1)} %broadcast_select_fusion.fact_ref.refs_0_, s32[3]{0:T(128)S(1)} %copy-done, bf16[4,128,512]{2,1,0:T(8,128)(2,1)S(1)} %pad_maximum_fusion.1.q_ref.refs_2_, ...), custom_call_target="tpu_custom_call" | custom-call | flops 5000000000 | bytes 4000000 | tf_op jit(solution)/shard_map/backward/pallas_call | solution.py:240
  93.3 1.0 collective-permute-start.17
  94.3 0.1 add_convert_fusion.2
  94.4 0.1 collective-permute-start.19
  94.5 0.0 collective-permute-done.20
  94.5 0.1 add_convert_fusion
  94.7 0.1 collective-permute-start.21
  94.8 1.5 %collective-permute-start.22 = (bf16[4,128,256]{2,1,0:T(8,128)(2,1)S(1)}, bf16[4,128,256]{2,1,0:T(8,128)(2,1)S(1)}, u32[]{:S(2)}, u32[]{:S(2)}) collective-permute-start(bf16[4,128,256]{2,1,0:T(8,128)(2,1)S(1)} %get-tuple-element.53), channel_id=1, source_target_pairs={{0,8},{8,16},{16,24},{24,0},{1,9},{9,17},{17,25},{25,1},{2,10},{10... | collective-permute-start | bytes 786440 | tf_op jit(solution)/shard_map/ppermute | solution.py:315
  96.2 0.1 slice_bitcast_fusion
  96.3 2.3 %collective-permute-start.13 = (bf16[128,1024]{1,0:T(8,128)(2,1)S(1)}, bf16[128,1024]{1,0:T(8,128)(2,1)S(1)}, u32[]{:S(2)}, u32[]{:S(2)}) collective-permute-start(bf16[128,1024]{1,0:T(8,128)(2,1)S(1)} %get-tuple-element.51), channel_id=1, source_target_pairs={{0,0},{1,32},{2,2},{3,34},{4,4},{5,36},{6,6},{7,38},{32,1},{33,33}... | collective-permute-start | bytes 786440 | tf_op jit(solution)/shard_map/ppermute | solution.py:310
  98.6 4.2 %collective-permute-start.14 = (bf16[128,1024]{1,0:T(8,128)(2,1)S(1)}, bf16[128,1024]{1,0:T(8,128)(2,1)S(1)}, u32[]{:S(2)}, u32[]{:S(2)}) collective-permute-start(bf16[128,1024]{1,0:T(8,128)(2,1)S(1)} %get-tuple-element.50), channel_id=1, source_target_pairs={{0,6},{1,38},{2,0},{3,32},{4,2},{5,34},{6,4},{7,36},{32,7},{33,39}... | collective-permute-start | bytes 786440 | tf_op jit(solution)/shard_map/ppermute | solution.py:310
  102.8 1.2 collective-permute-done.19
  103.9 1.4 %collective-permute-start.15 = (bf16[128,1024]{1,0:T(8,128)(2,1)S(1)}, bf16[128,1024]{1,0:T(8,128)(2,1)S(1)}, u32[]{:S(2)}, u32[]{:S(2)}) collective-permute-start(bf16[128,1024]{1,0:T(8,128)(2,1)S(1)} %get-tuple-element.49), channel_id=1, source_target_pairs={{0,4},{1,36},{2,6},{3,38},{4,0},{5,32},{6,2},{7,34},{32,5},{33,37}... | collective-permute-start | bytes 786440 | tf_op jit(solution)/shard_map/ppermute | solution.py:310
  105.4 2.1 %collective-permute-start.16 = (bf16[128,1024]{1,0:T(8,128)(2,1)S(1)}, bf16[128,1024]{1,0:T(8,128)(2,1)S(1)}, u32[]{:S(2)}, u32[]{:S(2)}) collective-permute-start(bf16[128,1024]{1,0:T(8,128)(2,1)S(1)} %get-tuple-element.48), channel_id=1, source_target_pairs={{0,2},{1,34},{2,4},{3,36},{4,6},{5,38},{6,0},{7,32},{32,3},{33,35}... | collective-permute-start | bytes 786440 | tf_op jit(solution)/shard_map/ppermute | solution.py:310
  107.4 2.4 %collective-permute-done.22 = bf16[4,128,256]{2,1,0:T(8,128)(2,1)S(1)} collective-permute-done((bf16[4,128,256]{2,1,0:T(8,128)(2,1)S(1)}, bf16[4,128,256]{2,1,0:T(8,128)(2,1)S(1)}, u32[]{:S(2)}, u32[]{:S(2)}) %collective-permute-start.22) | collective-permute-done | bytes 262176 | tf_op jit(solution)/shard_map/ppermute | solution.py:315
  109.8 0.2 add_convert_fusion.1
  110.0 1.9 %collective-permute-start.23 = (bf16[128,256]{1,0:T(8,128)(2,1)S(1)}, bf16[128,256]{1,0:T(8,128)(2,1)S(1)}, u32[]{:S(2)}, u32[]{:S(2)}) collective-permute-start(bf16[128,256]{1,0:T(8,128)(2,1)S(1)} %get-tuple-element.57), channel_id=1, source_target_pairs={{0,0},{1,32},{2,2},{3,34},{4,4},{5,36},{6,6},{7,38},{32,1},{33,33}... | collective-permute-start | bytes 196616 | tf_op jit(solution)/shard_map/ppermute | solution.py:310
  112.0 2.5 %collective-permute-done.13.refs_0_ = bf16[128,1024]{1,0:T(8,128)(2,1)S(1)} collective-permute-done((bf16[128,1024]{1,0:T(8,128)(2,1)S(1)}, bf16[128,1024]{1,0:T(8,128)(2,1)S(1)}, u32[]{:S(2)}, u32[]{:S(2)}) %collective-permute-start.13) | collective-permute-done | bytes 262176 | tf_op jit(solution)/shard_map/ppermute | solution.py:310
  114.5 0.1 collective-permute-done.14.refs_1_
  114.6 10.8 %collective-permute-start.25 = (bf16[128,256]{1,0:T(8,128)(2,1)S(1)}, bf16[128,256]{1,0:T(8,128)(2,1)S(1)}, u32[]{:S(2)}, u32[]{:S(2)}) collective-permute-start(bf16[128,256]{1,0:T(8,128)(2,1)S(1)} %get-tuple-element.55), channel_id=1, source_target_pairs={{0,4},{1,36},{2,6},{3,38},{4,0},{5,32},{6,2},{7,34},{32,5},{33,37}... | collective-permute-start | bytes 196616 | tf_op jit(solution)/shard_map/ppermute | solution.py:310
  125.5 4.3 %collective-permute-start.26 = (bf16[128,256]{1,0:T(8,128)(2,1)S(1)}, bf16[128,256]{1,0:T(8,128)(2,1)S(1)}, u32[]{:S(2)}, u32[]{:S(2)}) collective-permute-start(bf16[128,256]{1,0:T(8,128)(2,1)S(1)} %get-tuple-element.54), channel_id=1, source_target_pairs={{0,2},{1,34},{2,4},{3,36},{4,6},{5,38},{6,0},{7,32},{32,3},{33,35}... | collective-permute-start | bytes 196616 | tf_op jit(solution)/shard_map/ppermute | solution.py:310
  129.7 3.2 %collective-permute-done.16.refs_3_ = bf16[128,1024]{1,0:T(8,128)(2,1)S(1)} collective-permute-done((bf16[128,1024]{1,0:T(8,128)(2,1)S(1)}, bf16[128,1024]{1,0:T(8,128)(2,1)S(1)}, u32[]{:S(2)}, u32[]{:S(2)}) %collective-permute-start.16) | collective-permute-done | bytes 262176 | tf_op jit(solution)/shard_map/ppermute | solution.py:310
  132.9 3.7 %collective-permute-done.25.refs_6_ = bf16[128,256]{1,0:T(8,128)(2,1)S(1)} collective-permute-done((bf16[128,256]{1,0:T(8,128)(2,1)S(1)}, bf16[128,256]{1,0:T(8,128)(2,1)S(1)}, u32[]{:S(2)}, u32[]{:S(2)}) %collective-permute-start.25) | collective-permute-done | bytes 65568 | tf_op jit(solution)/shard_map/ppermute | solution.py:310
  136.7 0.6 copy-done.9
  137.3 0.6 copy-done.10
  137.9 2.4 %unpack.1 = (bf16[128,2048]{1,0:T(8,128)(2,1)}, bf16[128,2048]{1,0:T(8,128)(2,1)}, bf16[128,512]{1,0:T(8,128)(2,1)}, bf16[128,512]{1,0:T(8,128)(2,1)}) custom-call(s32[3]{0:T(128)} %pad_add_fusion.me_ref.refs_1_, bf16[128,1024]{1,0:T(8,128)(2,1)} %copy-done.3, bf16[128,1024]{1,0:T(8,128)(2,1)} %copy-done.4, bf16[128,1024]{1,0:T(8,128)(2,1)} %copy-done.5, ...), custom_call_target="tpu_custom_call" | custom-call | tf_op jit(solution)/shard_map/unpack/pallas_call | solution.py:294
  (36 shorter events, 0.2 us)
Async XLA Ops:
  3.4 15.2 %collective-permute-start = (bf16[128,768]{1,0:T(8,128)(2,1)}, bf16[128,768]{1,0:T(8,128)(2,1)S(1)}, u32[]{:S(2)}, u32[]{:S(2)}) collective-permute-start(bf16[128,768]{1,0:T(8,128)(2,1)} %get-tuple-element.26), channel_id=1, source_target_pairs={{0,0},{1,32},{2,2},{3,34},{4,4},{5,36},{6,6},{7,38},{32,1},{33,33}... | collective-permute-start | bytes 589832 | tf_op jit(solution)/shard_map/ppermute | solution.py:310
  7.5 14.5 %collective-permute-start.1 = (bf16[128,768]{1,0:T(8,128)(2,1)}, bf16[128,768]{1,0:T(8,128)(2,1)S(1)}, u32[]{:S(2)}, u32[]{:S(2)}) collective-permute-start(bf16[128,768]{1,0:T(8,128)(2,1)} %get-tuple-element.27), channel_id=1, source_target_pairs={{0,2},{1,34},{2,4},{3,36},{4,6},{5,38},{6,0},{7,32},{32,3},{33,35}... | collective-permute-start | bytes 589832 | tf_op jit(solution)/shard_map/ppermute | solution.py:310
  10.3 19.0 %collective-permute-start.2 = (bf16[128,768]{1,0:T(8,128)(2,1)}, bf16[128,768]{1,0:T(8,128)(2,1)S(1)}, u32[]{:S(2)}, u32[]{:S(2)}) collective-permute-start(bf16[128,768]{1,0:T(8,128)(2,1)} %get-tuple-element.28), channel_id=1, source_target_pairs={{0,4},{1,36},{2,6},{3,38},{4,0},{5,32},{6,2},{7,34},{32,5},{33,37}... | collective-permute-start | bytes 589832 | tf_op jit(solution)/shard_map/ppermute | solution.py:310
  14.2 23.7 %collective-permute-start.3 = (bf16[128,768]{1,0:T(8,128)(2,1)}, bf16[128,768]{1,0:T(8,128)(2,1)S(1)}, u32[]{:S(2)}, u32[]{:S(2)}) collective-permute-start(bf16[128,768]{1,0:T(8,128)(2,1)} %get-tuple-element.29), channel_id=1, source_target_pairs={{0,6},{1,38},{2,0},{3,32},{4,2},{5,34},{6,4},{7,36},{32,7},{33,39}... | collective-permute-start | bytes 589832 | tf_op jit(solution)/shard_map/ppermute | solution.py:310
  18.6 3.3 %copy-start.11 = (s32[4]{0:T(128)S(1)}, s32[4]{0:T(128)}, u32[]{:S(2)}) copy-start(s32[4]{0:T(128)} %param.10) | copy-start | bytes 52
  18.6 3.3 %copy-start.12 = (s32[32]{0:T(128)S(1)}, s32[32]{0:T(128)}, u32[]{:S(2)}) copy-start(s32[32]{0:T(128)} %param.11) | copy-start | bytes 388
  18.6 21.6 %collective-permute-start.10 = (bf16[128,512]{1,0:T(8,128)(2,1)}, bf16[128,512]{1,0:T(8,128)(2,1)S(1)}, u32[]{:S(2)}, u32[]{:S(2)}) collective-permute-start(bf16[128,512]{1,0:T(8,128)(2,1)} %get-tuple-element.33), channel_id=1, source_target_pairs={{0,6},{1,38},{2,0},{3,32},{4,2},{5,34},{6,4},{7,36},{32,7},{33,39}... | collective-permute-start | bytes 393224 | tf_op jit(solution)/shard_map/ppermute | solution.py:310
  18.7 24.0 %collective-permute-start.7 = (bf16[128,512]{1,0:T(8,128)(2,1)}, bf16[128,512]{1,0:T(8,128)(2,1)S(1)}, u32[]{:S(2)}, u32[]{:S(2)}) collective-permute-start(bf16[128,512]{1,0:T(8,128)(2,1)} %get-tuple-element.30), channel_id=1, source_target_pairs={{0,0},{1,32},{2,2},{3,34},{4,4},{5,36},{6,6},{7,38},{32,1},{33,33}... | collective-permute-start | bytes 393224 | tf_op jit(solution)/shard_map/ppermute | solution.py:310
  22.0 21.9 %collective-permute-start.8 = (bf16[128,512]{1,0:T(8,128)(2,1)}, bf16[128,512]{1,0:T(8,128)(2,1)S(1)}, u32[]{:S(2)}, u32[]{:S(2)}) collective-permute-start(bf16[128,512]{1,0:T(8,128)(2,1)} %get-tuple-element.31), channel_id=1, source_target_pairs={{0,2},{1,34},{2,4},{3,36},{4,6},{5,38},{6,0},{7,32},{32,3},{33,35}... | collective-permute-start | bytes 393224 | tf_op jit(solution)/shard_map/ppermute | solution.py:310
  29.3 14.6 %collective-permute-start.9 = (bf16[128,512]{1,0:T(8,128)(2,1)}, bf16[128,512]{1,0:T(8,128)(2,1)S(1)}, u32[]{:S(2)}, u32[]{:S(2)}) collective-permute-start(bf16[128,512]{1,0:T(8,128)(2,1)} %get-tuple-element.32), channel_id=1, source_target_pairs={{0,4},{1,36},{2,6},{3,38},{4,0},{5,32},{6,2},{7,34},{32,5},{33,37}... | collective-permute-start | bytes 393224 | tf_op jit(solution)/shard_map/ppermute | solution.py:310
  37.8 1.1 collective-permute-start.11
  39.0 8.9 %collective-permute-start.4 = (bf16[4,128,256]{2,1,0:T(8,128)(2,1)S(1)}, bf16[4,128,256]{2,1,0:T(8,128)(2,1)S(1)}, u32[]{:S(2)}, u32[]{:S(2)}) collective-permute-start(bf16[4,128,256]{2,1,0:T(8,128)(2,1)S(1)} %pad_maximum_fusion.5), channel_id=1, source_target_pairs={{0,8},{8,16},{16,24},{24,0},{1,9},{9,17},{17,25},{25,1},{2,10},{10... | collective-permute-start | bytes 786440 | tf_op jit(solution)/shard_map/ppermute | solution.py:315
  40.2 14.3 %collective-permute-start.5 = (bf16[4,128,256]{2,1,0:T(8,128)(2,1)S(1)}, bf16[4,128,256]{2,1,0:T(8,128)(2,1)S(1)}, u32[]{:S(2)}, u32[]{:S(2)}) collective-permute-start(bf16[4,128,256]{2,1,0:T(8,128)(2,1)S(1)} %pad_maximum_fusion.5), channel_id=1, source_target_pairs={{0,16},{8,24},{16,0},{24,8},{1,17},{9,25},{17,1},{25,9},{2,18},{10... | collective-permute-start | bytes 786440 | tf_op jit(solution)/shard_map/ppermute | solution.py:315
  42.6 12.4 %collective-permute-start.6 = (bf16[4,128,256]{2,1,0:T(8,128)(2,1)S(1)}, bf16[4,128,256]{2,1,0:T(8,128)(2,1)S(1)}, u32[]{:S(2)}, u32[]{:S(2)}) collective-permute-start(bf16[4,128,256]{2,1,0:T(8,128)(2,1)S(1)} %pad_maximum_fusion.5), channel_id=1, source_target_pairs={{0,24},{8,0},{16,8},{24,16},{1,25},{9,1},{17,9},{25,17},{2,26},{10... | collective-permute-start | bytes 786440 | tf_op jit(solution)/shard_map/ppermute | solution.py:315
  55.2 3.1 %copy-start = (s32[3]{0:T(128)S(1)}, s32[3]{0:T(128)}, u32[]{:S(2)}) copy-start(s32[3]{0:T(128)} %pad_add_fusion.me_ref.refs_1_) | copy-start | bytes 40
  55.2 3.1 %collective-permute-start.12 = (bf16[16,128,256]{2,1,0:T(8,128)(2,1)S(1)}, bf16[16,128,256]{2,1,0:T(8,128)(2,1)S(1)}, u32[]{:S(2)}, u32[]{:S(2)}) collective-permute-start(bf16[16,128,256]{2,1,0:T(8,128)(2,1)S(1)} %pad_maximum_fusion.own_ref.refs_5_.refs_6_), channel_id=1, source_target_pairs={{0,32},{32,0},{1,33},{33,1},{2,34},{34,2},{3,35},{35,3},{4,36},{36... | collective-permute-start | bytes 3145736 | tf_op jit(solution)/shard_map/ppermute | solution.py:319
  73.0 1.0 copy-start.2
  74.0 20.3 %collective-permute-start.18 = (bf16[4,128,256]{2,1,0:T(8,128)(2,1)S(1)}, bf16[4,128,256]{2,1,0:T(8,128)(2,1)S(1)}, u32[]{:S(2)}, u32[]{:S(2)}) collective-permute-start(bf16[4,128,256]{2,1,0:T(8,128)(2,1)S(1)} %get-tuple-element.45), channel_id=1, source_target_pairs={{0,32},{32,0},{1,33},{33,1},{2,34},{34,2},{3,35},{35,3},{4,36},{36... | collective-permute-start | bytes 786440 | tf_op jit(solution)/shard_map/ppermute | solution.py:319
  84.4 1.0 copy-start.1
  85.4 9.1 %collective-permute-start.20 = (bf16[8,128,256]{2,1,0:T(8,128)(2,1)S(1)}, bf16[8,128,256]{2,1,0:T(8,128)(2,1)S(1)}, u32[]{:S(2)}, u32[]{:S(2)}) collective-permute-start(bf16[8,128,256]{2,1,0:T(8,128)(2,1)S(1)} %get-tuple-element.47), channel_id=1, source_target_pairs={{0,32},{32,0},{1,33},{33,1},{2,34},{34,2},{3,35},{35,3},{4,36},{36... | collective-permute-start | bytes 1572872 | tf_op jit(solution)/shard_map/ppermute | solution.py:319
  93.3 5.3 %collective-permute-start.17 = (bf16[4,128,256]{2,1,0:T(8,128)(2,1)S(1)}, bf16[4,128,256]{2,1,0:T(8,128)(2,1)S(1)}, u32[]{:S(2)}, u32[]{:S(2)}) collective-permute-start(bf16[4,128,256]{2,1,0:T(8,128)(2,1)S(1)} %get-tuple-element.43), channel_id=1, source_target_pairs={{0,32},{32,0},{1,33},{33,1},{2,34},{34,2},{3,35},{35,3},{4,36},{36... | collective-permute-start | bytes 786440 | tf_op jit(solution)/shard_map/ppermute | solution.py:319
  94.4 9.5 %collective-permute-start.19 = (bf16[4,128,256]{2,1,0:T(8,128)(2,1)S(1)}, bf16[4,128,256]{2,1,0:T(8,128)(2,1)S(1)}, u32[]{:S(2)}, u32[]{:S(2)}) collective-permute-start(bf16[4,128,256]{2,1,0:T(8,128)(2,1)S(1)} %add_convert_fusion.2), channel_id=1, source_target_pairs={{0,16},{8,24},{16,0},{24,8},{1,17},{9,25},{17,1},{25,9},{2,18},{10... | collective-permute-start | bytes 786440 | tf_op jit(solution)/shard_map/ppermute | solution.py:315
  94.7 10.7 %collective-permute-start.21 = (bf16[4,128,256]{2,1,0:T(8,128)(2,1)S(1)}, bf16[4,128,256]{2,1,0:T(8,128)(2,1)S(1)}, u32[]{:S(2)}, u32[]{:S(2)}) collective-permute-start(bf16[4,128,256]{2,1,0:T(8,128)(2,1)S(1)} %get-tuple-element.52), channel_id=1, source_target_pairs={{0,24},{8,0},{16,8},{24,16},{1,25},{9,1},{17,9},{25,17},{2,26},{10... | collective-permute-start | bytes 786440 | tf_op jit(solution)/shard_map/ppermute | solution.py:315
  94.8 15.1 %collective-permute-start.22 = (bf16[4,128,256]{2,1,0:T(8,128)(2,1)S(1)}, bf16[4,128,256]{2,1,0:T(8,128)(2,1)S(1)}, u32[]{:S(2)}, u32[]{:S(2)}) collective-permute-start(bf16[4,128,256]{2,1,0:T(8,128)(2,1)S(1)} %get-tuple-element.53), channel_id=1, source_target_pairs={{0,8},{8,16},{16,24},{24,0},{1,9},{9,17},{17,25},{25,1},{2,10},{10... | collective-permute-start | bytes 786440 | tf_op jit(solution)/shard_map/ppermute | solution.py:315
  96.3 18.2 %collective-permute-start.13 = (bf16[128,1024]{1,0:T(8,128)(2,1)S(1)}, bf16[128,1024]{1,0:T(8,128)(2,1)S(1)}, u32[]{:S(2)}, u32[]{:S(2)}) collective-permute-start(bf16[128,1024]{1,0:T(8,128)(2,1)S(1)} %get-tuple-element.51), channel_id=1, source_target_pairs={{0,0},{1,32},{2,2},{3,34},{4,4},{5,36},{6,6},{7,38},{32,1},{33,33}... | collective-permute-start | bytes 786440 | tf_op jit(solution)/shard_map/ppermute | solution.py:310
  98.6 16.0 %collective-permute-start.14 = (bf16[128,1024]{1,0:T(8,128)(2,1)S(1)}, bf16[128,1024]{1,0:T(8,128)(2,1)S(1)}, u32[]{:S(2)}, u32[]{:S(2)}) collective-permute-start(bf16[128,1024]{1,0:T(8,128)(2,1)S(1)} %get-tuple-element.50), channel_id=1, source_target_pairs={{0,6},{1,38},{2,0},{3,32},{4,2},{5,34},{6,4},{7,36},{32,7},{33,39}... | collective-permute-start | bytes 786440 | tf_op jit(solution)/shard_map/ppermute | solution.py:310
  103.9 21.5 %collective-permute-start.15 = (bf16[128,1024]{1,0:T(8,128)(2,1)S(1)}, bf16[128,1024]{1,0:T(8,128)(2,1)S(1)}, u32[]{:S(2)}, u32[]{:S(2)}) collective-permute-start(bf16[128,1024]{1,0:T(8,128)(2,1)S(1)} %get-tuple-element.49), channel_id=1, source_target_pairs={{0,4},{1,36},{2,6},{3,38},{4,0},{5,32},{6,2},{7,34},{32,5},{33,37}... | collective-permute-start | bytes 786440 | tf_op jit(solution)/shard_map/ppermute | solution.py:310
  105.4 27.5 %collective-permute-start.16 = (bf16[128,1024]{1,0:T(8,128)(2,1)S(1)}, bf16[128,1024]{1,0:T(8,128)(2,1)S(1)}, u32[]{:S(2)}, u32[]{:S(2)}) collective-permute-start(bf16[128,1024]{1,0:T(8,128)(2,1)S(1)} %get-tuple-element.48), channel_id=1, source_target_pairs={{0,2},{1,34},{2,4},{3,36},{4,6},{5,38},{6,0},{7,32},{32,3},{33,35}... | collective-permute-start | bytes 786440 | tf_op jit(solution)/shard_map/ppermute | solution.py:310
  110.0 22.9 %collective-permute-start.23 = (bf16[128,256]{1,0:T(8,128)(2,1)S(1)}, bf16[128,256]{1,0:T(8,128)(2,1)S(1)}, u32[]{:S(2)}, u32[]{:S(2)}) collective-permute-start(bf16[128,256]{1,0:T(8,128)(2,1)S(1)} %get-tuple-element.57), channel_id=1, source_target_pairs={{0,0},{1,32},{2,2},{3,34},{4,4},{5,36},{6,6},{7,38},{32,1},{33,33}... | collective-permute-start | bytes 196616 | tf_op jit(solution)/shard_map/ppermute | solution.py:310
  114.5 22.1 %copy-start.3 = (bf16[128,1024]{1,0:T(8,128)(2,1)}, bf16[128,1024]{1,0:T(8,128)(2,1)S(1)}, u32[]{:S(2)}) copy-start(bf16[128,1024]{1,0:T(8,128)(2,1)S(1)} %collective-permute-done.13.refs_0_) | copy-start | bytes 786436
  114.5 18.4 %collective-permute-start.24 = (bf16[128,256]{1,0:T(8,128)(2,1)S(1)}, bf16[128,256]{1,0:T(8,128)(2,1)S(1)}, u32[]{:S(2)}, u32[]{:S(2)}) collective-permute-start(bf16[128,256]{1,0:T(8,128)(2,1)S(1)} %get-tuple-element.56), channel_id=1, source_target_pairs={{0,6},{1,38},{2,0},{3,32},{4,2},{5,34},{6,4},{7,36},{32,7},{33,39}... | collective-permute-start | bytes 196616 | tf_op jit(solution)/shard_map/ppermute | solution.py:310
  114.6 22.0 %copy-start.4 = (bf16[128,1024]{1,0:T(8,128)(2,1)}, bf16[128,1024]{1,0:T(8,128)(2,1)S(1)}, u32[]{:S(2)}) copy-start(bf16[128,1024]{1,0:T(8,128)(2,1)S(1)} %collective-permute-done.14.refs_1_) | copy-start | bytes 786436
  114.6 22.0 %collective-permute-start.25 = (bf16[128,256]{1,0:T(8,128)(2,1)S(1)}, bf16[128,256]{1,0:T(8,128)(2,1)S(1)}, u32[]{:S(2)}, u32[]{:S(2)}) collective-permute-start(bf16[128,256]{1,0:T(8,128)(2,1)S(1)} %get-tuple-element.55), channel_id=1, source_target_pairs={{0,4},{1,36},{2,6},{3,38},{4,0},{5,32},{6,2},{7,34},{32,5},{33,37}... | collective-permute-start | bytes 196616 | tf_op jit(solution)/shard_map/ppermute | solution.py:310
  125.4 11.2 %copy-start.5 = (bf16[128,1024]{1,0:T(8,128)(2,1)}, bf16[128,1024]{1,0:T(8,128)(2,1)S(1)}, u32[]{:S(2)}) copy-start(bf16[128,1024]{1,0:T(8,128)(2,1)S(1)} %collective-permute-done.15.refs_2_) | copy-start | bytes 786436
  125.5 11.2 %collective-permute-start.26 = (bf16[128,256]{1,0:T(8,128)(2,1)S(1)}, bf16[128,256]{1,0:T(8,128)(2,1)S(1)}, u32[]{:S(2)}, u32[]{:S(2)}) collective-permute-start(bf16[128,256]{1,0:T(8,128)(2,1)S(1)} %get-tuple-element.54), channel_id=1, source_target_pairs={{0,2},{1,34},{2,4},{3,36},{4,6},{5,38},{6,0},{7,32},{32,3},{33,35}... | collective-permute-start | bytes 196616 | tf_op jit(solution)/shard_map/ppermute | solution.py:310
  132.9 3.8 %copy-start.6 = (bf16[128,1024]{1,0:T(8,128)(2,1)}, bf16[128,1024]{1,0:T(8,128)(2,1)S(1)}, u32[]{:S(2)}) copy-start(bf16[128,1024]{1,0:T(8,128)(2,1)S(1)} %collective-permute-done.16.refs_3_) | copy-start | bytes 786436
  132.9 3.8 %copy-start.7 = (bf16[128,256]{1,0:T(8,128)(2,1)}, bf16[128,256]{1,0:T(8,128)(2,1)S(1)}, u32[]{:S(2)}) copy-start(bf16[128,256]{1,0:T(8,128)(2,1)S(1)} %collective-permute-done.23.refs_4_) | copy-start | bytes 196612
  132.9 3.8 %copy-start.8 = (bf16[128,256]{1,0:T(8,128)(2,1)}, bf16[128,256]{1,0:T(8,128)(2,1)S(1)}, u32[]{:S(2)}) copy-start(bf16[128,256]{1,0:T(8,128)(2,1)S(1)} %collective-permute-done.24.refs_5_) | copy-start | bytes 196612
  136.6 0.6 copy-start.9
  137.3 0.6 copy-start.10

commit v3 on v2

v3 whole, which is shorter than its diff:
```python
import jax
import jax.numpy as jnp
from jax import lax
from jax.experimental import pallas as pl
from jax.experimental.pallas import tpu as pltpu
from jax.sharding import Mesh, PartitionSpec as P

HEADS = 4
D = 128
B = 128
NX, NH, NL = 4, 4, 2
HEAD_AXIS, SEQ_AXIS = "zh", "x"
W = HEADS * B
SEEN = 18
STEP = 4
STEPS = (SEEN + 1 + STEP - 1) // STEP
SCALE = D ** -0.5
SCALE_LOG2 = SCALE * 1.4426950408889634
FILL = -1e30
BF, F32 = jnp.bfloat16, jnp.float32
VM = pl.BlockSpec(memory_space=pltpu.VMEM)
SM = pl.BlockSpec(memory_space=pltpu.SMEM)
ROOM = pltpu.CompilerParams(vmem_limit_bytes=48 * 2 ** 20)


def nt(a, b):
    return lax.dot_general(a, b, (((1,), (1,)), ((), ())), preferred_element_type=F32)


def tn(a, b):
    return lax.dot_general(a, b, (((0,), (0,)), ((), ())), preferred_element_type=F32)


def nn(a, b):
    return lax.dot_general(a, b, (((1,), (0,)), ((), ())), preferred_element_type=F32)


def sds(*shape, dtype=BF):
    return jax.ShapeDtypeStruct(shape, dtype)


class Places:
    def __init__(self, fact_ref, me_ref, shifts, table_ref, list_ref):
        self.fact_ref, self.me_ref = fact_ref, me_ref
        self.table_ref, self.list_ref = table_ref, list_ref
        self.count = 2 * NH * len(shifts)
        self.ends = []
        total = jnp.int32(0)
        for i in range(4):
            total = total + fact_ref[NX * NH * NL + i]
            self.ends.append(total)
        for k, dx in enumerate(shifts):
            for side in range(2):
                for step in range(NH):
                    table_ref[(k * 2 + side) * NH + step] = self.span(dx, step, side)

    def span(self, dx, step, side):
        e, seq, head = self.me_ref[0], self.me_ref[1], self.me_ref[2]
        from_x = lax.rem(seq + NX - dx, NX)
        from_zh = lax.rem(head + NH - step, NH)
        return self.fact_ref[(from_x * NH + from_zh) * NL + lax.rem(e + side, NL)]

    def of_query_block(self, i):
        span = self.span(0, i, 0)
        first = span * B
        self.q_pos = first + lax.rem(lax.broadcasted_iota(jnp.int32, (1, W), 1), B)
        self.q_start = jnp.zeros((1, W), jnp.int32)
        start_first = jnp.int32(0)
        for e in self.ends:
            start_first = jnp.where(e <= first, e, start_first)
            self.q_start = jnp.where(e <= self.q_pos, e, self.q_start)
        self.low, self.high = start_first // B, span

    def listed(self, n, entries):
        for j in entries:
            s = self.table_ref[j]
            self.list_ref[0, n] = j
            self.list_ref[1, n] = s * B
            n = n + jnp.where((s >= self.low) & (s <= self.high), 1, 0)
        return n

    def padded(self, n):
        for j in range(STEP):
            self.list_ref[0, n + j] = 0
            self.list_ref[1, n + j] = SEEN * B * 4

    def blocks(self, at, number):
        return [self.list_ref[0, at + j] for j in range(number)]

    def mask(self, at, number):
        row = lax.broadcasted_iota(jnp.int32, (B, W), 0)
        parts = []
        for j in range(number):
            k_pos = row + self.list_ref[1, at + j]
            parts.append((k_pos >= self.q_start) & (k_pos <= self.q_pos))
        return jnp.concatenate(parts, axis=0)


def stacked(ref, i, which):
    return jnp.concatenate(
        [ref[i, :, (which * HEADS + h) * D:(which * HEADS + h + 1) * D] for h in range(HEADS)], axis=0
    )


def taken(ref, blocks, cols):
    return jnp.concatenate([ref[block, :, cols] for block in blocks], axis=0)


SHIFTS = (1, 2, 3, 0)
EARLY = (2,)
FAR = 2 * NH * (NX - 1)
KEYS, VALUES = slice(0, D), slice(D, 2 * D)


def gradients(dqt, keys, p, dp, delta, qs, dos, acc_ref, blocks):
    ds = (p * (dp - delta)).astype(BF)
    dv = nn(p.astype(BF), dos)
    dk = nn(ds, qs)
    for j, block in enumerate(blocks):
        acc_ref[block, :, KEYS] += dk[j * B:(j + 1) * B]
        acc_ref[block, :, VALUES] += dv[j * B:(j + 1) * B]
    return dqt + tn(keys, ds)


def put_gradients(own_out, sib_out, acc_ref):
    for ref, side in ((own_out, 0), (sib_out, 1)):
        for j in range(ref.shape[0]):
            at = (j // NH * 2 + side) * NH + j % NH
            ref[j, :, KEYS] = (acc_ref[at, :, KEYS] * SCALE).astype(BF)
            ref[j, :, VALUES] = acc_ref[at, :, VALUES].astype(BF)


def far_kernel(fact_ref, me_ref, qdo_ref, own_ref, sib_ref,
               o_ref, stat_ref, own_out, sib_out, dqt_out,
               s_ref, kv_ref, acc_ref, table_ref, list_ref):
    for k, dx in enumerate(SHIFTS):
        kv_ref[2 * k * NH:(2 * k + 1) * NH] = own_ref[dx * NH:(dx + 1) * NH]
        kv_ref[(2 * k + 1) * NH:(2 * k + 2) * NH] = sib_ref[dx * NH:(dx + 1) * NH]
    places = Places(fact_ref, me_ref, SHIFTS, table_ref, list_ref)
    acc_ref[...] = jnp.zeros_like(acc_ref)

    def one_block(i, carry):
        places.of_query_block(i)
        far = places.listed(jnp.int32(0), range(FAR))
        list_ref[0, far] = 0
        list_ref[1, far] = SEEN * B * 4
        far = (far + 1) // 2 * 2
        n = places.listed(far, range(FAR, 2 * NX * NH))
        places.padded(n)
        steps = (n + STEP - 1) // STEP
        qs, dos = stacked(qdo_ref, i, 0), stacked(qdo_ref, i, 1)

        def score_step(c, m):
            blocks = places.blocks(STEP * c, STEP)
            st = nt(taken(kv_ref, blocks, KEYS), qs) * SCALE_LOG2
            st = jnp.where(places.mask(STEP * c, STEP), st, FILL)
            s_ref[c] = st
            return jnp.maximum(m, jnp.max(st.reshape(-1, 8, W), axis=0))

        m = lax.fori_loop(0, steps, score_step, jnp.full((8, W), FILL, F32))
        m = jnp.max(m, axis=0, keepdims=True)

        def weigh_step(c, state):
            l, ot = state
            blocks = places.blocks(STEP * c, STEP)
            p = jnp.exp2(s_ref[c] - m)
            return (
                l + jnp.sum(p.reshape(-1, 8, W), axis=0),
                ot + tn(taken(kv_ref, blocks, VALUES), p.astype(BF)),
            )

        state = jnp.zeros((8, W), F32), jnp.zeros((D, W), F32)
        l, ot = lax.fori_loop(0, steps, weigh_step, state)
        l = jnp.sum(l, axis=0, keepdims=True)
        ob = (ot * (1.0 / l)).astype(BF)
        delta = []
        for h in range(HEADS):
            cols = slice(h * B, (h + 1) * B)
            of = ob[:, cols].astype(F32)
            o_ref[i, :, cols] = of.T.astype(BF)
            dot = qdo_ref[i, :, W + h * B:W + (h + 1) * B].astype(F32).T
            delta.append(jnp.sum(of * dot, axis=0, keepdims=True))
        delta = jnp.concatenate(delta, axis=1)
        lse = m + jnp.log2(l)
        stat_ref[i, 0:1, :] = lse
        stat_ref[i, 1:2, :] = delta

        def back_step(c, part, number, dqt):
            at = STEP * c + part
            blocks = places.blocks(at, number)
            p = jnp.exp2(s_ref[c, part * B:(part + number) * B] - lse)
            dp = nt(taken(kv_ref, blocks, VALUES), dos)
            keys = taken(kv_ref, blocks, KEYS)
            return gradients(dqt, keys, p, dp, delta, qs, dos, acc_ref, blocks)

        wide = far // STEP
        dqt = lax.fori_loop(
            0, wide, lambda c, t: back_step(c, 0, STEP, t), jnp.zeros((D, W), F32)
        )
        dqt_out[i] = lax.fori_loop(
            wide, (far + STEP - 1) // STEP, lambda c, t: back_step(c, 0, STEP // 2, t), dqt
        )
        return carry

    lax.fori_loop(0, NH, one_block, 0)
    put_gradients(own_out, sib_out, acc_ref)


def far(facts, me, qdo, own, sib):
    blocks = 2 * NX * NH
    return pl.pallas_call(
        far_kernel,
        in_specs=[SM] * 2 + [VM] * 3,
        out_specs=[VM] * 5,
        out_shape=[sds(NH, B, W), sds(NH, 8, W, dtype=F32)]
        + [sds(FAR // 2, B, 2 * D)] * 2 + [sds(NH, D, W, dtype=F32)],
        scratch_shapes=[
            pltpu.VMEM((STEPS, STEP * B, W), F32),
            pltpu.VMEM((blocks, B, 2 * D), BF),
            pltpu.VMEM((FAR, B, 2 * D), F32),
            pltpu.SMEM((blocks,), jnp.int32),
            pltpu.SMEM((2, blocks + 8), jnp.int32),
        ],
        compiler_params=ROOM,
        cost_estimate=pl.CostEstimate(flops=20 * 10 ** 9, bytes_accessed=4 * 10 ** 6, transcendentals=0),
        name="far",
    )(facts, me, qdo, own, sib)


def near_kernel(fact_ref, me_ref, qdo_ref, stat_ref, own_ref, sib_ref, dqt_ref,
                own_out, sib_out, dq_ref, kv_ref, acc_ref, table_ref, list_ref):
    kv_ref[:NH] = own_ref[...]
    kv_ref[NH:] = sib_ref[...]
    places = Places(fact_ref, me_ref, (0,), table_ref, list_ref)
    acc_ref[...] = jnp.zeros_like(acc_ref)

    def one_block(i, carry):
        places.of_query_block(i)
        n = places.listed(jnp.int32(0), range(2 * NH))
        places.padded(n)
        qs, dos = stacked(qdo_ref, i, 0), stacked(qdo_ref, i, 1)
        lse, delta = stat_ref[i, 0:1, :], stat_ref[i, 1:2, :]

        def step(at, number, dqt):
            blocks = places.blocks(at, number)
            keys = taken(kv_ref, blocks, KEYS)
            st = nt(keys, qs) * SCALE_LOG2 - lse
            p = jnp.exp2(jnp.where(places.mask(at, number), st, FILL))
            dp = nt(taken(kv_ref, blocks, VALUES), dos)
            return gradients(dqt, keys, p, dp, delta, qs, dos, acc_ref, blocks)

        wide = (n + 1) // STEP
        dqt = lax.fori_loop(0, wide, lambda c, t: step(STEP * c, STEP, t), dqt_ref[i])
        dqt = lax.fori_loop(
            wide, (n + STEP - 1) // STEP, lambda c, t: step(STEP * c, STEP // 2, t), dqt
        )
        for h in range(HEADS):
            cols = slice(h * B, (h + 1) * B)
            dq_ref[i, :, cols] = (dqt[:, cols] * SCALE).T.astype(BF)
        return carry

    lax.fori_loop(0, NH, one_block, 0)
    put_gradients(own_out, sib_out, acc_ref)


def near(facts, me, qdo, stat, own, sib, dqt):
    chunk = pl.BlockSpec((NH, B, 2 * D), lambda g: (0, 0, 0))
    return pl.pallas_call(
        near_kernel,
        grid=(1,),
        in_specs=[SM] * 2 + [VM] * 2 + [chunk] * 2 + [VM],
        out_specs=[VM] * 3,
        out_shape=[sds(NH, B, 2 * D)] * 2 + [sds(NH, B, W)],
        scratch_shapes=[
            pltpu.VMEM((2 * NH, B, 2 * D), BF),
            pltpu.VMEM((2 * NH, B, 2 * D), F32),
            pltpu.SMEM((2 * NH,), jnp.int32),
            pltpu.SMEM((2, 2 * NH + 8), jnp.int32),
        ],
        compiler_params=ROOM,
        cost_estimate=pl.CostEstimate(flops=7 * 10 ** 9, bytes_accessed=4 * 10 ** 6, transcendentals=0),
        name="near",
    )(facts, me, qdo, stat, own, sib, dqt)


def pack_kernel(me_ref, *refs):
    arrays, outs = refs[:-NH], refs[-NH:]
    for s, out in enumerate(outs):
        group, at = lax.rem(me_ref[2] + s, NH), 0
        for ref in arrays:
            width = ref.shape[1] // NH
            out[:, at:at + width] = ref[:, pl.ds(pl.multiple_of(group * width, width), width)]
            at += width


def pack(me, *arrays):
    width = sum(a.shape[1] for a in arrays) // NH
    return pl.pallas_call(
        pack_kernel,
        in_specs=[SM] + [VM] * len(arrays),
        out_specs=[VM] * NH,
        out_shape=[sds(B, width)] * NH,
        name="pack",
    )(me, *arrays)


def unpack_kernel(me_ref, *refs):
    early, late, outs = refs[:len(EARLY)], refs[len(EARLY):-4], refs[-4:]
    for s in range(NH):
        group = lax.rem(me_ref[2] + s, NH)
        wide = pl.ds(pl.multiple_of(group * W, W), W)
        narrow = pl.ds(pl.multiple_of(group * D, D), D)
        if s in EARLY:
            outs[0][:, wide] = early[EARLY.index(s)][...]
        else:
            outs[0][:, wide] = late[s][:, 2 * D + W:]
        outs[1][:, wide] = late[s][:, 2 * D:2 * D + W]
        outs[2][:, narrow] = late[s][:, KEYS]
        outs[3][:, narrow] = late[s][:, VALUES]


def unpack(me, early, late):
    return pl.pallas_call(
        unpack_kernel,
        in_specs=[SM] + [VM] * (len(EARLY) + NH),
        out_specs=[VM] * 4,
        out_shape=[sds(B, NH * W)] * 2 + [sds(B, NH * D)] * 2,
        name="unpack",
    )(me, *[early[s] for s in EARLY], *late)


def by_heads(piece, s, sign):
    perm = [
        ((c * NH + h) * NL + l, (l * NH + (h + sign * s) % NH) * NL + c)
        for c in range(2) for h in range(NH) for l in range(NL)
    ]
    return lax.ppermute(piece, ("core", HEAD_AXIS, "zl"), perm)


def to_seq(array, shift):
    return lax.ppermute(array, SEQ_AXIS, [(i, (i + shift) % NX) for i in range(NX)])


def to_sibling(array):
    return lax.ppermute(array, "core", [(0, 1), (1, 0)])


def on_device(queries, key_vectors, value_vectors, output_cotangent, doc_lengths, span_of):
    core, zl = lax.axis_index("core"), lax.axis_index("zl")
    me = jnp.stack([core, lax.axis_index(SEQ_AXIS), lax.axis_index(HEAD_AXIS)]).astype(jnp.int32)
    kv = pack(me, key_vectors, value_vectors)
    kv = jnp.stack([by_heads(kv[s], s, 1) for s in range(NH)])
    qdo = pack(me, queries, output_cotangent)
    qdo = jnp.stack([by_heads(qdo[s], s, 1) for s in range(NH)])
    facts = jnp.concatenate([span_of, doc_lengths])
    facts = jnp.where(core == zl, facts, to_sibling(facts))
    own = jnp.concatenate([kv] + [to_seq(kv, dx) for dx in range(1, NX)])
    own, qdo, facts = lax.optimization_barrier((own, qdo, facts))
    sib = to_sibling(own)
    o, stat, mine, theirs, dqt = far(facts, me, qdo, own, sib)

    def added(mine, theirs):
        return mine.astype(F32) + to_sibling(theirs).astype(F32)

    sums = added(mine, theirs).astype(BF)
    early = {s: by_heads(o[s], s, -1) for s in EARLY}
    dqt, sums = lax.optimization_barrier((dqt, sums))
    mine0, theirs0, dq = near(facts, me, qdo, stat, own, sib, dqt)
    came = [to_seq(sums[k * NH:(k + 1) * NH], -dx) for k, dx in enumerate(SHIFTS[:-1])]
    theirs0, came, early = lax.optimization_barrier((theirs0, came, early))
    total = added(mine0, theirs0)
    for part in came:
        total = total + part.astype(F32)
    total = total.astype(BF)
    late = [
        jnp.concatenate([total[s], dq[s]] + ([] if s in EARLY else [o[s]]), axis=1)
        for s in range(NH)
    ]
    late = [by_heads(late[s], s, -1) for s in range(NH)]
    return unpack(me, early, late)


def solution(mesh):
    split = Mesh(
        mesh.devices.reshape(-1, 2, NX, NH, NL), ("y", "core", "x", "zh", "zl")
    )
    rows = P(("y", "core", "x", "zh", "zl"), None)
    part = P(("y", "core"))
    return jax.shard_map(
        on_device,
        mesh=split,
        in_specs=(rows, rows, rows, rows, part, part),
        out_specs=(rows, rows, rows, rows),
        check_vma=False,
    )
```

time: 141 us -> 129 us (0.915)
  the two profiles are of different devices: /device:TPU:17 before, /device:TPU:1 now
where the time goes in v3:
time: 129 us; the launch traced here: 130 us
  starting transfers between devices  45 us (35%)
  waiting for transfers between devices  42.3 us (33%)
  Pallas kernels  36.9 us (29%)
  local copies, waits for them, and re-layouts  2.85 us (2%)
  other arithmetic  2.2 us (2%)
    ppermute x13, waiting for transfers between devices, by_heads(): return lax.ppermute(piece, ('core', HEAD_AXIS, 'zl'), perm)  31.6 us
    ppermute x13, starting transfers between devices, by_heads(): return lax.ppermute(piece, ('core', HEAD_AXIS, 'zl'), perm)  27.6 us
    pallas_call x1, Pallas kernels, far(): pl.pallas_call(far_kernel, in_specs=[SM] * 2 + [VM] * 3, out_specs=[VM] *...  25.8 us
    ppermute x6, starting transfers between devices, to_seq(): lax.ppermute(array, SEQ_AXIS, [(i, (i + shift) % NX) for i in range(NX)])  11.2 us
    ppermute x4, starting transfers between devices, to_sibling(): return lax.ppermute(array, 'core', [(0, 1), (1, 0)])  6.15 us
    ppermute x6, waiting for transfers between devices, to_seq(): lax.ppermute(array, SEQ_AXIS, [(i, (i + shift) % NX) for i in range(NX)])  5.37 us
    ppermute x4, waiting for transfers between devices, to_sibling(): return lax.ppermute(array, 'core', [(0, 1), (1, 0)])  5.36 us
    pallas_call x1, Pallas kernels, near(): pl.pallas_call(near_kernel, grid=(1,), in_specs=[SM] * 2 + [VM] * 2 + [ch...  4.66 us
  transfers between devices with their start and end apart: 23, of which 11 were waited for; matrix products, arithmetic and copies ran while one was open for 1% of the time, Pallas kernels for 7%

profile of v3, /device:TPU:1, one launch (start us, length us, event | category | flops | bytes accessed | tf_op | source)
XLA Modules:
  0.0 130.2 jit_solution(8576470308660932255)
XLA Ops:
  0.7 0.8 pad_add_fusion.1
  1.4 3.3 %collective-permute-start.11 = (s32[36]{0:T(128)S(1)}, s32[36]{0:T(128)S(1)}, u32[]{:S(2)}, u32[]{:S(2)}) collective-permute-start(s32[36]{0:T(128)S(1)} %pad_add_fusion.1), channel_id=1, source_target_pairs={{0,32},{32,0},{1,33},{33,1},{2,34},{34,2},{3,35},{35,3},{4,36},{36... | collective-permute-start | bytes 440 | tf_op jit(solution)/shard_map/ppermute | solution.py:345
  4.7 0.7 pad_add_fusion.me_ref
  5.4 1.7 %pack.2 = (bf16[128,256]{1,0:T(8,128)(2,1)}, bf16[128,256]{1,0:T(8,128)(2,1)}, bf16[128,256]{1,0:T(8,128)(2,1)}, bf16[128,256]{1,0:T(8,128)(2,1)}) custom-call(s32[3]{0:T(128)} %pad_add_fusion.me_ref, bf16[128,512]{1,0:T(8,128)(2,1)} %refs_0_.2, bf16[128,512]{1,0:T(8,128)(2,1)} %refs_1_.2), custom_call_target="tpu_custom_call" | custom-call | tf_op jit(solution)/shard_map/pack/pallas_call | solution.py:298
  7.1 1.9 %collective-permute-start = (bf16[128,256]{1,0:T(8,128)(2,1)}, bf16[128,256]{1,0:T(8,128)(2,1)S(1)}, u32[]{:S(2)}, u32[]{:S(2)}) collective-permute-start(bf16[128,256]{1,0:T(8,128)(2,1)} %get-tuple-element.30), channel_id=1, source_target_pairs={{0,0},{1,32},{2,2},{3,34},{4,4},{5,36},{6,6},{7,38},{32,1},{33,33}... | collective-permute-start | bytes 196616 | tf_op jit(solution)/shard_map/ppermute | solution.py:337
  9.0 2.8 %collective-permute-start.1 = (bf16[128,256]{1,0:T(8,128)(2,1)}, bf16[128,256]{1,0:T(8,128)(2,1)S(1)}, u32[]{:S(2)}, u32[]{:S(2)}) collective-permute-start(bf16[128,256]{1,0:T(8,128)(2,1)} %get-tuple-element.31), channel_id=1, source_target_pairs={{0,2},{1,34},{2,4},{3,36},{4,6},{5,38},{6,0},{7,32},{32,3},{33,35}... | collective-permute-start | bytes 196616 | tf_op jit(solution)/shard_map/ppermute | solution.py:337
  11.8 3.7 %collective-permute-start.2 = (bf16[128,256]{1,0:T(8,128)(2,1)}, bf16[128,256]{1,0:T(8,128)(2,1)S(1)}, u32[]{:S(2)}, u32[]{:S(2)}) collective-permute-start(bf16[128,256]{1,0:T(8,128)(2,1)} %get-tuple-element.32), channel_id=1, source_target_pairs={{0,4},{1,36},{2,6},{3,38},{4,0},{5,32},{6,2},{7,34},{32,5},{33,37}... | collective-permute-start | bytes 196616 | tf_op jit(solution)/shard_map/ppermute | solution.py:337
  15.4 3.2 %collective-permute-start.3 = (bf16[128,256]{1,0:T(8,128)(2,1)}, bf16[128,256]{1,0:T(8,128)(2,1)S(1)}, u32[]{:S(2)}, u32[]{:S(2)}) collective-permute-start(bf16[128,256]{1,0:T(8,128)(2,1)} %get-tuple-element.33), channel_id=1, source_target_pairs={{0,6},{1,38},{2,0},{3,32},{4,2},{5,34},{6,4},{7,36},{32,7},{33,39}... | collective-permute-start | bytes 196616 | tf_op jit(solution)/shard_map/ppermute | solution.py:337
  18.6 2.3 %pack.3 = (bf16[128,1024]{1,0:T(8,128)(2,1)}, bf16[128,1024]{1,0:T(8,128)(2,1)}, bf16[128,1024]{1,0:T(8,128)(2,1)}, bf16[128,1024]{1,0:T(8,128)(2,1)}) custom-call(s32[3]{0:T(128)} %pad_add_fusion.me_ref, bf16[128,2048]{1,0:T(8,128)(2,1)} %refs_0_.3, bf16[128,2048]{1,0:T(8,128)(2,1)} %refs_1_.3), custom_call_target="tpu_custom_call" | custom-call | tf_op jit(solution)/shard_map/pack/pallas_call | solution.py:298
  20.9 0.0 collective-permute-done.11
  20.9 2.5 %collective-permute-start.7 = (bf16[128,1024]{1,0:T(8,128)(2,1)}, bf16[128,1024]{1,0:T(8,128)(2,1)S(1)}, u32[]{:S(2)}, u32[]{:S(2)}) collective-permute-start(bf16[128,1024]{1,0:T(8,128)(2,1)} %get-tuple-element.34), channel_id=1, source_target_pairs={{0,0},{1,32},{2,2},{3,34},{4,4},{5,36},{6,6},{7,38},{32,1},{33,33}... | collective-permute-start | bytes 786440 | tf_op jit(solution)/shard_map/ppermute | solution.py:337
  23.5 0.1 broadcast_select_fusion.fact_ref
  23.6 0.0 collective-permute-done
  23.6 0.8 collective-permute-start.8
  24.4 0.0 collective-permute-done.1
  24.4 1.2 collective-permute-start.9
  25.6 0.0 collective-permute-done.2
  25.6 2.2 %collective-permute-start.10 = (bf16[128,1024]{1,0:T(8,128)(2,1)}, bf16[128,1024]{1,0:T(8,128)(2,1)S(1)}, u32[]{:S(2)}, u32[]{:S(2)}) collective-permute-start(bf16[128,1024]{1,0:T(8,128)(2,1)} %get-tuple-element.37), channel_id=1, source_target_pairs={{0,6},{1,38},{2,0},{3,32},{4,2},{5,34},{6,4},{7,36},{32,7},{33,39}... | collective-permute-start | bytes 786440 | tf_op jit(solution)/shard_map/ppermute | solution.py:337
  27.8 0.0 collective-permute-done.3
  27.9 2.8 %collective-permute-start.5 = (bf16[4,128,256]{2,1,0:T(8,128)(2,1)S(1)}, bf16[4,128,256]{2,1,0:T(8,128)(2,1)S(1)}, u32[]{:S(2)}, u32[]{:S(2)}) collective-permute-start(bf16[4,128,256]{2,1,0:T(8,128)(2,1)S(1)} %pad_maximum_fusion.4), channel_id=1, source_target_pairs={{0,16},{8,24},{16,0},{24,8},{1,17},{9,25},{17,1},{25,9},{2,18},{10... | collective-permute-start | bytes 786440 | tf_op jit(solution)/shard_map/ppermute | solution.py:341
  30.7 4.1 %collective-permute-done.7 = bf16[128,1024]{1,0:T(8,128)(2,1)S(1)} collective-permute-done((bf16[128,1024]{1,0:T(8,128)(2,1)}, bf16[128,1024]{1,0:T(8,128)(2,1)S(1)}, u32[]{:S(2)}, u32[]{:S(2)}) %collective-permute-start.7) | collective-permute-done | bytes 262176 | tf_op jit(solution)/shard_map/ppermute | solution.py:337
  34.8 1.2 collective-permute-start.4
  36.1 3.0 %collective-permute-done.8 = bf16[128,1024]{1,0:T(8,128)(2,1)S(1)} collective-permute-done((bf16[128,1024]{1,0:T(8,128)(2,1)}, bf16[128,1024]{1,0:T(8,128)(2,1)S(1)}, u32[]{:S(2)}, u32[]{:S(2)}) %collective-permute-start.8) | collective-permute-done | bytes 262176 | tf_op jit(solution)/shard_map/ppermute | solution.py:337
  39.1 2.5 %collective-permute-start.6 = (bf16[4,128,256]{2,1,0:T(8,128)(2,1)S(1)}, bf16[4,128,256]{2,1,0:T(8,128)(2,1)S(1)}, u32[]{:S(2)}, u32[]{:S(2)}) collective-permute-start(bf16[4,128,256]{2,1,0:T(8,128)(2,1)S(1)} %pad_maximum_fusion.4), channel_id=1, source_target_pairs={{0,24},{8,0},{16,8},{24,16},{1,25},{9,1},{17,9},{25,17},{2,26},{10... | collective-permute-start | bytes 786440 | tf_op jit(solution)/shard_map/ppermute | solution.py:341
  41.6 2.4 %collective-permute-done.9 = bf16[128,1024]{1,0:T(8,128)(2,1)S(1)} collective-permute-done((bf16[128,1024]{1,0:T(8,128)(2,1)}, bf16[128,1024]{1,0:T(8,128)(2,1)S(1)}, u32[]{:S(2)}, u32[]{:S(2)}) %collective-permute-start.9) | collective-permute-done | bytes 262176 | tf_op jit(solution)/shard_map/ppermute | solution.py:337
  43.9 3.7 %collective-permute-done.10 = bf16[128,1024]{1,0:T(8,128)(2,1)S(1)} collective-permute-done((bf16[128,1024]{1,0:T(8,128)(2,1)}, bf16[128,1024]{1,0:T(8,128)(2,1)S(1)}, u32[]{:S(2)}, u32[]{:S(2)}) %collective-permute-start.10) | collective-permute-done | bytes 262176 | tf_op jit(solution)/shard_map/ppermute | solution.py:337
  47.6 0.1 pad_maximum_fusion.qdo_ref
  47.8 0.0 copy-start
  47.8 0.0 collective-permute-done.4
  47.8 0.0 collective-permute-done.5
  47.8 0.0 collective-permute-done.6
  47.9 1.4 %collective-permute-start.12 = (bf16[16,128,256]{2,1,0:T(8,128)(2,1)S(1)}, bf16[16,128,256]{2,1,0:T(8,128)(2,1)S(1)}, u32[]{:S(2)}, u32[]{:S(2)}) collective-permute-start(bf16[16,128,256]{2,1,0:T(8,128)(2,1)S(1)} %constant_dynamic-update-slice_fusion.own_ref), channel_id=1, source_target_pairs={{0,32},{32,0},{1,33},{33,1},{2,34},{34,2},{3,35},{35,3},{4,36},{36... | collective-permute-start | bytes 3145736 | tf_op jit(solution)/shard_map/ppermute | solution.py:345
  49.2 2.3 %collective-permute-done.12.sib_ref = bf16[16,128,256]{2,1,0:T(8,128)(2,1)S(1)} collective-permute-done((bf16[16,128,256]{2,1,0:T(8,128)(2,1)S(1)}, bf16[16,128,256]{2,1,0:T(8,128)(2,1)S(1)}, u32[]{:S(2)}, u32[]{:S(2)}) %collective-permute-start.12) | collective-permute-done | bytes 1048608 | tf_op jit(solution)/shard_map/ppermute | solution.py:345
  51.5 1.0 copy-done.1
  52.5 25.8 %far.1 = (bf16[4,128,512]{2,1,0:T(8,128)(2,1)S(1)}, f32[4,8,512]{2,1,0:T(8,128)S(1)}, bf16[12,128,256]{2,1,0:T(8,128)(2,1)S(1)}, bf16[12,128,256]{2,1,0:T(8,128)(2,1)S(1)}, f32[4,128,512]{2,1,0:T(8,128)S(1)}) custom-call(s32[36]{0:T(128)S(1)} %broadcast_select_fusion.fact_ref, s32[3]{0:T(128)S(1)} %copy-done, ...), custom_call_target="tpu_custom_call" | custom-call | flops 20000000000 | bytes 4000000 | tf_op jit(solution)/shard_map/far/pallas_call | solution.py:211
  78.3 0.1 collective-permute-start.13
  78.5 0.3 collective-permute-start.17
  78.7 1.9 %collective-permute-done.13 = bf16[12,128,256]{2,1,0:T(8,128)(2,1)S(1)} collective-permute-done((bf16[12,128,256]{2,1,0:T(8,128)(2,1)S(1)}, bf16[12,128,256]{2,1,0:T(8,128)(2,1)S(1)}, u32[]{:S(2)}, u32[]{:S(2)}) %collective-permute-start.13) | collective-permute-done | bytes 786464 | tf_op jit(solution)/shard_map/ppermute | solution.py:345
  80.7 0.2 add_convert_fusion
  80.9 0.1 fusion
  81.0 2.2 %collective-permute-start.16 = (bf16[4,128,256]{2,1,0:T(8,128)(2,1)S(1)}, bf16[4,128,256]{2,1,0:T(8,128)(2,1)S(1)}, u32[]{:S(2)}, u32[]{:S(2)}) collective-permute-start(bf16[4,128,256]{2,1,0:T(8,128)(2,1)S(1)} %get-tuple-element.56), channel_id=1, source_target_pairs={{0,8},{8,16},{16,24},{24,0},{1,9},{9,17},{17,25},{25,1},{2,10},{10... | collective-permute-start | bytes 786440 | tf_op jit(solution)/shard_map/ppermute | solution.py:341
  83.2 0.0 collective-permute-start.15
  83.2 2.5 %collective-permute-start.14 = (bf16[4,128,256]{2,1,0:T(8,128)(2,1)S(1)}, bf16[4,128,256]{2,1,0:T(8,128)(2,1)S(1)}, u32[]{:S(2)}, u32[]{:S(2)}) collective-permute-start(bf16[4,128,256]{2,1,0:T(8,128)(2,1)S(1)} %get-tuple-element.58), channel_id=1, source_target_pairs={{0,24},{8,0},{16,8},{24,16},{1,25},{9,1},{17,9},{25,17},{2,26},{10... | collective-permute-start | bytes 786440 | tf_op jit(solution)/shard_map/ppermute | solution.py:341
  85.7 4.7 %near.1 = (bf16[4,128,256]{2,1,0:T(8,128)(2,1)S(1)}, bf16[4,128,256]{2,1,0:T(8,128)(2,1)S(1)}, bf16[4,128,512]{2,1,0:T(8,128)(2,1)S(1)}) custom-call(s32[36]{0:T(128)S(1)} %broadcast_select_fusion.fact_ref, s32[3]{0:T(128)S(1)} %copy-done, bf16[4,128,1024]{2,1,0:T(8,128)(2,1)S(1)} %pad_maximum_fusion.qdo_ref, f32[4,8,512]{2,1,0:T(8,128)S(1)} %get-tuple-element.41.stat_ref, ...), custom_call_target="tpu_custom_call" | custom-call | flops 7000000000 | bytes 4000000 | tf_op jit(solution)/shard_map/near/pallas_call | solution.py:268
  90.4 0.0 collective-permute-done.17.refs_0_
  90.4 3.9 %collective-permute-done.16 = bf16[4,128,256]{2,1,0:T(8,128)(2,1)S(1)} collective-permute-done((bf16[4,128,256]{2,1,0:T(8,128)(2,1)S(1)}, bf16[4,128,256]{2,1,0:T(8,128)(2,1)S(1)}, u32[]{:S(2)}, u32[]{:S(2)}) %collective-permute-start.16) | collective-permute-done | bytes 262176 | tf_op jit(solution)/shard_map/ppermute | solution.py:341
  94.3 0.1 collective-permute-done.15
  94.4 1.4 %collective-permute-done.14 = bf16[4,128,256]{2,1,0:T(8,128)(2,1)S(1)} collective-permute-done((bf16[4,128,256]{2,1,0:T(8,128)(2,1)S(1)}, bf16[4,128,256]{2,1,0:T(8,128)(2,1)S(1)}, u32[]{:S(2)}, u32[]{:S(2)}) %collective-permute-start.14) | collective-permute-done | bytes 262176 | tf_op jit(solution)/shard_map/ppermute | solution.py:341
  95.8 1.4 %collective-permute-start.18 = (bf16[4,128,256]{2,1,0:T(8,128)(2,1)S(1)}, bf16[4,128,256]{2,1,0:T(8,128)(2,1)S(1)}, u32[]{:S(2)}, u32[]{:S(2)}) collective-permute-start(bf16[4,128,256]{2,1,0:T(8,128)(2,1)S(1)} %get-tuple-element.51), channel_id=1, source_target_pairs={{0,32},{32,0},{1,33},{33,1},{2,34},{34,2},{3,35},{35,3},{4,36},{36... | collective-permute-start | bytes 786440 | tf_op jit(solution)/shard_map/ppermute | solution.py:345
  97.3 1.1 collective-permute-done.18
  98.4 0.2 add_convert_fusion.1
  98.6 2.5 %collective-permute-start.19 = (bf16[128,1280]{1,0:T(8,128)(2,1)S(1)}, bf16[128,1280]{1,0:T(8,128)(2,1)S(1)}, u32[]{:S(2)}, u32[]{:S(2)}) collective-permute-start(bf16[128,1280]{1,0:T(8,128)(2,1)S(1)} %pad_maximum_fusion.1), channel_id=1, source_target_pairs={{0,0},{1,32},{2,2},{3,34},{4,4},{5,36},{6,6},{7,38},{32,1},{33,33}... | collective-permute-start | bytes 983048 | tf_op jit(solution)/shard_map/ppermute | solution.py:337
  101.2 2.5 %collective-permute-start.20 = (bf16[128,1280]{1,0:T(8,128)(2,1)S(1)}, bf16[128,1280]{1,0:T(8,128)(2,1)S(1)}, u32[]{:S(2)}, u32[]{:S(2)}) collective-permute-start(bf16[128,1280]{1,0:T(8,128)(2,1)S(1)} %pad_maximum_fusion.2), channel_id=1, source_target_pairs={{0,6},{1,38},{2,0},{3,32},{4,2},{5,34},{6,4},{7,36},{32,7},{33,39}... | collective-permute-start | bytes 983048 | tf_op jit(solution)/shard_map/ppermute | solution.py:337
  103.7 1.8 %collective-permute-start.22 = (bf16[128,1280]{1,0:T(8,128)(2,1)S(1)}, bf16[128,1280]{1,0:T(8,128)(2,1)S(1)}, u32[]{:S(2)}, u32[]{:S(2)}) collective-permute-start(bf16[128,1280]{1,0:T(8,128)(2,1)S(1)} %pad_maximum_fusion.3), channel_id=1, source_target_pairs={{0,2},{1,34},{2,4},{3,36},{4,6},{5,38},{6,0},{7,32},{32,3},{33,35}... | collective-permute-start | bytes 983048 | tf_op jit(solution)/shard_map/ppermute | solution.py:337
  105.5 2.2 %collective-permute-start.21 = (bf16[128,768]{1,0:T(8,128)(2,1)S(1)}, bf16[128,768]{1,0:T(8,128)(2,1)S(1)}, u32[]{:S(2)}, u32[]{:S(2)}) collective-permute-start(bf16[128,768]{1,0:T(8,128)(2,1)S(1)} %pad_maximum_fusion.5), channel_id=1, source_target_pairs={{0,4},{1,36},{2,6},{3,38},{4,0},{5,32},{6,2},{7,34},{32,5},{33,37}... | collective-permute-start | bytes 589832 | tf_op jit(solution)/shard_map/ppermute | solution.py:337
  107.7 18.4 %collective-permute-done.21.refs_3_ = bf16[128,768]{1,0:T(8,128)(2,1)S(1)} collective-permute-done((bf16[128,768]{1,0:T(8,128)(2,1)S(1)}, bf16[128,768]{1,0:T(8,128)(2,1)S(1)}, u32[]{:S(2)}, u32[]{:S(2)}) %collective-permute-start.21) | collective-permute-done | bytes 196640 | tf_op jit(solution)/shard_map/ppermute | solution.py:337
  126.1 0.0 collective-permute-done.19.refs_1_
  126.1 0.0 collective-permute-done.20.refs_2_
  126.1 0.0 collective-permute-done.22.refs_4_
  126.1 0.7 copy-done.6
  126.8 0.1 copy-done.3
  126.9 0.1 copy-done.4
  127.0 0.7 copy-done.5
  127.7 2.5 %unpack.1 = (bf16[128,2048]{1,0:T(8,128)(2,1)}, bf16[128,2048]{1,0:T(8,128)(2,1)}, bf16[128,512]{1,0:T(8,128)(2,1)}, bf16[128,512]{1,0:T(8,128)(2,1)}) custom-call(s32[3]{0:T(128)} %pad_add_fusion.me_ref, bf16[128,512]{1,0:T(8,128)(2,1)} %copy-done.7, bf16[128,1280]{1,0:T(8,128)(2,1)} %copy-done.3, bf16[128,1280]{1,0:T(8,128)(2,1)} %copy-done.4, ...), custom_call_target="tpu_custom_call" | custom-call | tf_op jit(solution)/shard_map/unpack/pallas_call | solution.py:323
  (29 shorter events, 0.3 us)
Async XLA Ops:
  0.6 22.8 %copy-start.9 = (s32[32]{0:T(128)S(1)}, s32[32]{0:T(128)}, u32[]{:S(2)}) copy-start(s32[32]{0:T(128)} %param.11) | copy-start | bytes 388
  0.6 22.8 %copy-start.8 = (s32[4]{0:T(128)S(1)}, s32[4]{0:T(128)}, u32[]{:S(2)}) copy-start(s32[4]{0:T(128)} %param.10) | copy-start | bytes 52
  1.4 19.5 %collective-permute-start.11 = (s32[36]{0:T(128)S(1)}, s32[36]{0:T(128)S(1)}, u32[]{:S(2)}, u32[]{:S(2)}) collective-permute-start(s32[36]{0:T(128)S(1)} %pad_add_fusion.1), channel_id=1, source_target_pairs={{0,32},{32,0},{1,33},{33,1},{2,34},{34,2},{3,35},{35,3},{4,36},{36... | collective-permute-start | bytes 440 | tf_op jit(solution)/shard_map/ppermute | solution.py:345
  7.1 16.5 %collective-permute-start = (bf16[128,256]{1,0:T(8,128)(2,1)}, bf16[128,256]{1,0:T(8,128)(2,1)S(1)}, u32[]{:S(2)}, u32[]{:S(2)}) collective-permute-start(bf16[128,256]{1,0:T(8,128)(2,1)} %get-tuple-element.30), channel_id=1, source_target_pairs={{0,0},{1,32},{2,2},{3,34},{4,4},{5,36},{6,6},{7,38},{32,1},{33,33}... | collective-permute-start | bytes 196616 | tf_op jit(solution)/shard_map/ppermute | solution.py:337
  9.0 15.4 %collective-permute-start.1 = (bf16[128,256]{1,0:T(8,128)(2,1)}, bf16[128,256]{1,0:T(8,128)(2,1)S(1)}, u32[]{:S(2)}, u32[]{:S(2)}) collective-permute-start(bf16[128,256]{1,0:T(8,128)(2,1)} %get-tuple-element.31), channel_id=1, source_target_pairs={{0,2},{1,34},{2,4},{3,36},{4,6},{5,38},{6,0},{7,32},{32,3},{33,35}... | collective-permute-start | bytes 196616 | tf_op jit(solution)/shard_map/ppermute | solution.py:337
  11.8 13.8 %collective-permute-start.2 = (bf16[128,256]{1,0:T(8,128)(2,1)}, bf16[128,256]{1,0:T(8,128)(2,1)S(1)}, u32[]{:S(2)}, u32[]{:S(2)}) collective-permute-start(bf16[128,256]{1,0:T(8,128)(2,1)} %get-tuple-element.32), channel_id=1, source_target_pairs={{0,4},{1,36},{2,6},{3,38},{4,0},{5,32},{6,2},{7,34},{32,5},{33,37}... | collective-permute-start | bytes 196616 | tf_op jit(solution)/shard_map/ppermute | solution.py:337
  15.4 12.4 %collective-permute-start.3 = (bf16[128,256]{1,0:T(8,128)(2,1)}, bf16[128,256]{1,0:T(8,128)(2,1)S(1)}, u32[]{:S(2)}, u32[]{:S(2)}) collective-permute-start(bf16[128,256]{1,0:T(8,128)(2,1)} %get-tuple-element.33), channel_id=1, source_target_pairs={{0,6},{1,38},{2,0},{3,32},{4,2},{5,34},{6,4},{7,36},{32,7},{33,39}... | collective-permute-start | bytes 196616 | tf_op jit(solution)/shard_map/ppermute | solution.py:337
  20.9 13.9 %collective-permute-start.7 = (bf16[128,1024]{1,0:T(8,128)(2,1)}, bf16[128,1024]{1,0:T(8,128)(2,1)S(1)}, u32[]{:S(2)}, u32[]{:S(2)}) collective-permute-start(bf16[128,1024]{1,0:T(8,128)(2,1)} %get-tuple-element.34), channel_id=1, source_target_pairs={{0,0},{1,32},{2,2},{3,34},{4,4},{5,36},{6,6},{7,38},{32,1},{33,33}... | collective-permute-start | bytes 786440 | tf_op jit(solution)/shard_map/ppermute | solution.py:337
  23.6 15.5 %collective-permute-start.8 = (bf16[128,1024]{1,0:T(8,128)(2,1)}, bf16[128,1024]{1,0:T(8,128)(2,1)S(1)}, u32[]{:S(2)}, u32[]{:S(2)}) collective-permute-start(bf16[128,1024]{1,0:T(8,128)(2,1)} %get-tuple-element.35), channel_id=1, source_target_pairs={{0,2},{1,34},{2,4},{3,36},{4,6},{5,38},{6,0},{7,32},{32,3},{33,35}... | collective-permute-start | bytes 786440 | tf_op jit(solution)/shard_map/ppermute | solution.py:337
  24.4 19.6 %collective-permute-start.9 = (bf16[128,1024]{1,0:T(8,128)(2,1)}, bf16[128,1024]{1,0:T(8,128)(2,1)S(1)}, u32[]{:S(2)}, u32[]{:S(2)}) collective-permute-start(bf16[128,1024]{1,0:T(8,128)(2,1)} %get-tuple-element.36), channel_id=1, source_target_pairs={{0,4},{1,36},{2,6},{3,38},{4,0},{5,32},{6,2},{7,34},{32,5},{33,37}... | collective-permute-start | bytes 786440 | tf_op jit(solution)/shard_map/ppermute | solution.py:337
  25.6 22.0 %collective-permute-start.10 = (bf16[128,1024]{1,0:T(8,128)(2,1)}, bf16[128,1024]{1,0:T(8,128)(2,1)S(1)}, u32[]{:S(2)}, u32[]{:S(2)}) collective-permute-start(bf16[128,1024]{1,0:T(8,128)(2,1)} %get-tuple-element.37), channel_id=1, source_target_pairs={{0,6},{1,38},{2,0},{3,32},{4,2},{5,34},{6,4},{7,36},{32,7},{33,39}... | collective-permute-start | bytes 786440 | tf_op jit(solution)/shard_map/ppermute | solution.py:337
  27.9 19.9 %collective-permute-start.5 = (bf16[4,128,256]{2,1,0:T(8,128)(2,1)S(1)}, bf16[4,128,256]{2,1,0:T(8,128)(2,1)S(1)}, u32[]{:S(2)}, u32[]{:S(2)}) collective-permute-start(bf16[4,128,256]{2,1,0:T(8,128)(2,1)S(1)} %pad_maximum_fusion.4), channel_id=1, source_target_pairs={{0,16},{8,24},{16,0},{24,8},{1,17},{9,25},{17,1},{25,9},{2,18},{10... | collective-permute-start | bytes 786440 | tf_op jit(solution)/shard_map/ppermute | solution.py:341
  34.8 12.9 %collective-permute-start.4 = (bf16[4,128,256]{2,1,0:T(8,128)(2,1)S(1)}, bf16[4,128,256]{2,1,0:T(8,128)(2,1)S(1)}, u32[]{:S(2)}, u32[]{:S(2)}) collective-permute-start(bf16[4,128,256]{2,1,0:T(8,128)(2,1)S(1)} %pad_maximum_fusion.4), channel_id=1, source_target_pairs={{0,8},{8,16},{16,24},{24,0},{1,9},{9,17},{17,25},{25,1},{2,10},{10... | collective-permute-start | bytes 786440 | tf_op jit(solution)/shard_map/ppermute | solution.py:341
  39.1 8.8 %collective-permute-start.6 = (bf16[4,128,256]{2,1,0:T(8,128)(2,1)S(1)}, bf16[4,128,256]{2,1,0:T(8,128)(2,1)S(1)}, u32[]{:S(2)}, u32[]{:S(2)}) collective-permute-start(bf16[4,128,256]{2,1,0:T(8,128)(2,1)S(1)} %pad_maximum_fusion.4), channel_id=1, source_target_pairs={{0,24},{8,0},{16,8},{24,16},{1,25},{9,1},{17,9},{25,17},{2,26},{10... | collective-permute-start | bytes 786440 | tf_op jit(solution)/shard_map/ppermute | solution.py:341
  47.8 4.7 %copy-start = (s32[3]{0:T(128)S(1)}, s32[3]{0:T(128)}, u32[]{:S(2)}) copy-start(s32[3]{0:T(128)} %pad_add_fusion.me_ref) | copy-start | bytes 40
  47.9 3.6 %collective-permute-start.12 = (bf16[16,128,256]{2,1,0:T(8,128)(2,1)S(1)}, bf16[16,128,256]{2,1,0:T(8,128)(2,1)S(1)}, u32[]{:S(2)}, u32[]{:S(2)}) collective-permute-start(bf16[16,128,256]{2,1,0:T(8,128)(2,1)S(1)} %constant_dynamic-update-slice_fusion.own_ref), channel_id=1, source_target_pairs={{0,32},{32,0},{1,33},{33,1},{2,34},{34,2},{3,35},{35,3},{4,36},{36... | collective-permute-start | bytes 3145736 | tf_op jit(solution)/shard_map/ppermute | solution.py:345
  51.5 1.0 copy-start.1
  78.3 2.4 %collective-permute-start.13 = (bf16[12,128,256]{2,1,0:T(8,128)(2,1)S(1)}, bf16[12,128,256]{2,1,0:T(8,128)(2,1)S(1)}, u32[]{:S(2)}, u32[]{:S(2)}) collective-permute-start(bf16[12,128,256]{2,1,0:T(8,128)(2,1)S(1)} %get-tuple-element.44), channel_id=1, source_target_pairs={{0,32},{32,0},{1,33},{33,1},{2,34},{34,2},{3,35},{35,3},{4,36},{36... | collective-permute-start | bytes 2359304 | tf_op jit(solution)/shard_map/ppermute | solution.py:345
  78.5 11.9 %collective-permute-start.17 = (bf16[128,512]{1,0:T(8,128)(2,1)S(1)}, bf16[128,512]{1,0:T(8,128)(2,1)S(1)}, u32[]{:S(2)}, u32[]{:S(2)}) collective-permute-start(bf16[128,512]{1,0:T(8,128)(2,1)S(1)} %get-tuple-element.66), channel_id=1, source_target_pairs={{0,4},{1,36},{2,6},{3,38},{4,0},{5,32},{6,2},{7,34},{32,5},{33,37}... | collective-permute-start | bytes 393224 | tf_op jit(solution)/shard_map/ppermute | solution.py:337
  80.9 4.8 %copy-start.2 = (bf16[16,128,256]{2,1,0:T(8,128)(2,1)S(1)}, bf16[16,128,256]{2,1,0:T(8,128)(2,1)}, u32[]{:S(2)}) copy-start(bf16[16,128,256]{2,1,0:T(8,128)(2,1)} %copy-done.1) | copy-start | bytes 3145732
  81.0 13.3 %collective-permute-start.16 = (bf16[4,128,256]{2,1,0:T(8,128)(2,1)S(1)}, bf16[4,128,256]{2,1,0:T(8,128)(2,1)S(1)}, u32[]{:S(2)}, u32[]{:S(2)}) collective-permute-start(bf16[4,128,256]{2,1,0:T(8,128)(2,1)S(1)} %get-tuple-element.56), channel_id=1, source_target_pairs={{0,8},{8,16},{16,24},{24,0},{1,9},{9,17},{17,25},{25,1},{2,10},{10... | collective-permute-start | bytes 786440 | tf_op jit(solution)/shard_map/ppermute | solution.py:341
  83.2 11.2 %collective-permute-start.15 = (bf16[4,128,256]{2,1,0:T(8,128)(2,1)S(1)}, bf16[4,128,256]{2,1,0:T(8,128)(2,1)S(1)}, u32[]{:S(2)}, u32[]{:S(2)}) collective-permute-start(bf16[4,128,256]{2,1,0:T(8,128)(2,1)S(1)} %get-tuple-element.57), channel_id=1, source_target_pairs={{0,16},{8,24},{16,0},{24,8},{1,17},{9,25},{17,1},{25,9},{2,18},{10... | collective-permute-start | bytes 786440 | tf_op jit(solution)/shard_map/ppermute | solution.py:341
  83.2 12.5 %collective-permute-start.14 = (bf16[4,128,256]{2,1,0:T(8,128)(2,1)S(1)}, bf16[4,128,256]{2,1,0:T(8,128)(2,1)S(1)}, u32[]{:S(2)}, u32[]{:S(2)}) collective-permute-start(bf16[4,128,256]{2,1,0:T(8,128)(2,1)S(1)} %get-tuple-element.58), channel_id=1, source_target_pairs={{0,24},{8,0},{16,8},{24,16},{1,25},{9,1},{17,9},{25,17},{2,26},{10... | collective-permute-start | bytes 786440 | tf_op jit(solution)/shard_map/ppermute | solution.py:341
  90.4 8.2 %copy-start.7 = (bf16[128,512]{1,0:T(8,128)(2,1)}, bf16[128,512]{1,0:T(8,128)(2,1)S(1)}, u32[]{:S(2)}) copy-start(bf16[128,512]{1,0:T(8,128)(2,1)S(1)} %collective-permute-done.17.refs_0_) | copy-start | bytes 393220
  95.8 2.6 %collective-permute-start.18 = (bf16[4,128,256]{2,1,0:T(8,128)(2,1)S(1)}, bf16[4,128,256]{2,1,0:T(8,128)(2,1)S(1)}, u32[]{:S(2)}, u32[]{:S(2)}) collective-permute-start(bf16[4,128,256]{2,1,0:T(8,128)(2,1)S(1)} %get-tuple-element.51), channel_id=1, source_target_pairs={{0,32},{32,0},{1,33},{33,1},{2,34},{34,2},{3,35},{35,3},{4,36},{36... | collective-permute-start | bytes 786440 | tf_op jit(solution)/shard_map/ppermute | solution.py:345
  98.6 27.4 %collective-permute-start.19 = (bf16[128,1280]{1,0:T(8,128)(2,1)S(1)}, bf16[128,1280]{1,0:T(8,128)(2,1)S(1)}, u32[]{:S(2)}, u32[]{:S(2)}) collective-permute-start(bf16[128,1280]{1,0:T(8,128)(2,1)S(1)} %pad_maximum_fusion.1), channel_id=1, source_target_pairs={{0,0},{1,32},{2,2},{3,34},{4,4},{5,36},{6,6},{7,38},{32,1},{33,33}... | collective-permute-start | bytes 983048 | tf_op jit(solution)/shard_map/ppermute | solution.py:337
  101.2 24.9 %collective-permute-start.20 = (bf16[128,1280]{1,0:T(8,128)(2,1)S(1)}, bf16[128,1280]{1,0:T(8,128)(2,1)S(1)}, u32[]{:S(2)}, u32[]{:S(2)}) collective-permute-start(bf16[128,1280]{1,0:T(8,128)(2,1)S(1)} %pad_maximum_fusion.2), channel_id=1, source_target_pairs={{0,6},{1,38},{2,0},{3,32},{4,2},{5,34},{6,4},{7,36},{32,7},{33,39}... | collective-permute-start | bytes 983048 | tf_op jit(solution)/shard_map/ppermute | solution.py:337
  103.7 22.4 %collective-permute-start.22 = (bf16[128,1280]{1,0:T(8,128)(2,1)S(1)}, bf16[128,1280]{1,0:T(8,128)(2,1)S(1)}, u32[]{:S(2)}, u32[]{:S(2)}) collective-permute-start(bf16[128,1280]{1,0:T(8,128)(2,1)S(1)} %pad_maximum_fusion.3), channel_id=1, source_target_pairs={{0,2},{1,34},{2,4},{3,36},{4,6},{5,38},{6,0},{7,32},{32,3},{33,35}... | collective-permute-start | bytes 983048 | tf_op jit(solution)/shard_map/ppermute | solution.py:337
  105.5 20.6 %collective-permute-start.21 = (bf16[128,768]{1,0:T(8,128)(2,1)S(1)}, bf16[128,768]{1,0:T(8,128)(2,1)S(1)}, u32[]{:S(2)}, u32[]{:S(2)}) collective-permute-start(bf16[128,768]{1,0:T(8,128)(2,1)S(1)} %pad_maximum_fusion.5), channel_id=1, source_target_pairs={{0,4},{1,36},{2,6},{3,38},{4,0},{5,32},{6,2},{7,34},{32,5},{33,37}... | collective-permute-start | bytes 589832 | tf_op jit(solution)/shard_map/ppermute | solution.py:337
  126.1 0.7 copy-start.6
  126.1 0.8 copy-start.3
  126.1 0.9 copy-start.4
  127.0 0.7 copy-start.5
